TPU v7x, 256 devices: a whole 4x4x8 slice. The times are simulated.
256 devices in a mesh: inst: 32 (over z, y), tp: 8 (over x, core).
Axes of the slice: x: 4, y: 4, z: 8, core: 2. Of those that a mesh axis runs over, the one named last changes fastest.
Arguments:
- caches: bfloat16 [2, 128, 512, 1024], P(None, 'inst', None, 'tp'), may hold values from -6 to 6
- queries: bfloat16 [2, 128, 8192], P(None, 'inst', 'tp'), may hold values from -140 to 140
- new_entries: bfloat16 [2, 2, 128, 1024], P(None, None, 'inst', 'tp'), may hold values from -6 to 6
- lengths: int32 [128], replicated, may hold values from 2 to 510, as said below
- targets: int32 [128], replicated, may hold values from 0 to 127, as said below
- output_weight: bfloat16 [8192, 5120], P('tp'), may hold values from -0.375 to 0.375
Outputs:
- step_one_out: bfloat16 [128, 5120], P('inst', 'tp')
- step_two_out: bfloat16 [128, 5120], P('inst', 'tp')
- caches_after: bfloat16 [2, 128, 512, 1024], P(None, 'inst', None, 'tp')
Inputs may be any that keep to these rules, and one draw needn't show every extreme that they name: `lengths`: some request has exactly 510. `targets`: a permutation of the 128 slots (slot i * 4 + j is slot j of instance i); from every instance exactly 2 requests move to other instances and every other request keeps its slot; for each k the k-th leaving request (in slot order) of every instance moves the same number of instances forward along inst, cyclically; one of these two numbers is 1 and the other 16.
All inputs are finite; a program needn't handle non-finite values.
Results may differ from a plain program's by a relative error of at most 0.022.
Values may be sent and summed in bfloat16 or wider, within the bound.
No kernel may reach another device: no remote copies, remote signals or barrier semaphores. Data moves between devices by JAX's collectives and lax.ppermute only.
A program may use at most 128 MiB of HBM per device.

v0:
```python
import jax
import jax.numpy as jnp
from jax import lax
from jax.sharding import PartitionSpec as P

HD = 128
MOVE = 2


def write_token(stored, entries, lengths_now):
    positions = lax.broadcasted_iota(jnp.int32, (1, stored.shape[1], stored.shape[2], 1), 2)
    at_length = positions == lengths_now[None, :, None, None]
    return jnp.where(at_length, entries[:, :, None, :], stored)


def attend(stored, query, lengths_now):
    slot_count, capacity, features = (stored.shape[1], stored.shape[2], stored.shape[3])
    kv_heads = features // HD
    group_size = query.shape[1] // features
    grouped_query = query.reshape(slot_count, kv_heads, group_size, HD)
    key_rows = stored[0].reshape(slot_count, capacity, kv_heads, HD)
    value_rows = stored[1].reshape(slot_count, capacity, kv_heads, HD)
    scores = jnp.einsum(
        "skgd,sckd->skgc", grouped_query, key_rows, preferred_element_type=jnp.float32
    ) * HD ** (-0.5)
    visible = jnp.arange(capacity, dtype=jnp.int32)[None, :] <= lengths_now[:, None]
    scores = jnp.where(visible[:, None, None, :], scores, -jnp.inf)
    row_max = jnp.max(scores, axis=-1, keepdims=True)
    weights = jnp.exp(scores - row_max)
    weights_bf = (weights / jnp.sum(weights, axis=-1, keepdims=True)).astype(jnp.bfloat16)
    weighted = jnp.einsum(
        "skgc,sckd->skgd", weights_bf, value_rows, preferred_element_type=jnp.float32
    )
    return weighted.reshape(slot_count, kv_heads * group_size * HD).astype(jnp.bfloat16)


def head_term(attended, output_weight):
    return lax.dot_general(
        output_weight, attended, (((0,), (1,)), ((), ())), preferred_element_type=jnp.float32
    )


def project_each(attended, output_weight):
    summed = lax.psum_scatter(
        head_term(attended, output_weight).astype(jnp.bfloat16),
        "tp",
        scatter_dimension=0,
        tiled=True,
    ).astype(jnp.float32)
    return summed.T.astype(jnp.bfloat16)


def on_device(caches, queries, new_entries, lengths, targets, output_weight):
    slot_count = caches.shape[1]
    groups = lax.axis_size("inst")
    own_index = lax.axis_index("inst")
    first_slot = own_index * slot_count
    slot_ids = jnp.arange(slot_count, dtype=jnp.int32)
    lengths_old = lax.dynamic_slice_in_dim(lengths, first_slot, slot_count)
    caches_one = write_token(caches, new_entries[0], lengths_old)
    att_one = attend(caches_one, queries[0], lengths_old)
    everyone = jnp.arange(targets.shape[0], dtype=jnp.int32)
    source = jnp.zeros_like(targets).at[targets].set(everyone)
    src_local = lax.dynamic_slice_in_dim(source, first_slot, slot_count)
    src_inst = src_local // slot_count
    lengths_two = jnp.take(lengths, src_local) + 1
    own_targets = lax.dynamic_slice_in_dim(targets, first_slot, slot_count)
    target_inst = own_targets // slot_count
    leaving = target_inst != own_index
    step_query = queries[1][None]
    step_new = new_entries[1]
    moving_flags = (targets // slot_count != everyone // slot_count).astype(jnp.int32)
    ranking_all = (jnp.cumsum(moving_flags.reshape(groups, slot_count), axis=1) - 1).reshape(-1)
    ranking = jnp.cumsum(leaving.astype(jnp.int32)) - 1
    rank_match = leaving[None, :] & (ranking[None, :] == jnp.arange(MOVE, dtype=jnp.int32)[:, None])
    leaver_slots = jnp.sum(jnp.where(rank_match, slot_ids[None, :], 0), axis=1)
    send_caches = jnp.take(caches_one, leaver_slots, axis=1)
    send_query = jnp.take(step_query, leaver_slots, axis=1)
    send_new = jnp.take(step_new, leaver_slots, axis=1)
    arrived = (
        lax.all_gather(send_caches, "inst", axis=1, tiled=True),
        lax.all_gather(send_query, "inst", axis=1, tiled=True),
        lax.all_gather(send_new, "inst", axis=1, tiled=True),
    )
    remote_index = src_inst * MOVE + jnp.take(ranking_all, src_local)
    staying = src_inst == own_index
    local_index = jnp.where(staying, src_local - first_slot, 0)
    remote_index = jnp.where(staying, 0, remote_index)
    locals_kept = (caches_one, step_query, step_new)
    relocated = []
    for member_local, member_remote in zip(locals_kept, arrived):
        chosen_shape = (1, slot_count) + (1,) * (member_local.ndim - 2)
        staying_mask = staying.reshape(chosen_shape)
        relocated.append(
            jnp.where(
                staying_mask,
                jnp.take(member_local, local_index, axis=1),
                jnp.take(member_remote, remote_index, axis=1),
            )
        )
    caches_after = write_token(relocated[0], relocated[2], lengths_two)
    att_two = attend(caches_after, relocated[1][0], lengths_two)
    step_one_out = project_each(att_one, output_weight)
    step_two_out = project_each(att_two, output_weight)
    return (step_one_out, step_two_out, caches_after)


def solution(mesh):
    placed = (
        P(None, "inst", None, "tp"),
        P(None, "inst", "tp"),
        P(None, None, "inst", "tp"),
        P(),
        P(),
        P("tp", None),
    )
    return jax.shard_map(
        on_device,
        mesh=mesh,
        in_specs=placed,
        out_specs=(P("inst", "tp"), P("inst", "tp"), P(None, "inst", None, "tp")),
        check_vma=False,
    )
```

profile of v0, /device:TPU:24, one launch (start us, length us, event | category | flops | bytes accessed | tf_op | source)
XLA Modules:
  0.0 214.3 jit_solution(8106570656977289205)
XLA Ops:
  8.0 0.0 all-gather.2.cloned.1.call-start
  8.0 0.7 convert_bitcast_fusion
  8.8 0.2 reduce-window.8
  9.0 0.1 fusion.30
  9.1 0.7 dynamic_slice.9
  9.9 0.1 iota_compare_fusion.3
  9.9 0.7 fusion.39
  10.6 1.5 broadcast_select_fusion
  12.1 0.6 gather_fusion.7
  12.8 0.9 select_bitcast_fusion
  13.7 0.0 copy-start.1
  13.7 0.0 all-gather.2.cloned.1.call-update
  13.7 0.0 reduce-scatter.7.cloned.1.call-start
  13.8 0.7 slice_bitcast_fusion.8
  14.5 0.4 fusion.40
  14.9 0.3 fusion.11
  15.2 0.0 copy-start
  15.2 5.5 %fusion.2 = bf16[5120,4]{0,1:T(4,128)(2,1)S(1)} fusion(bf16[1024,5120]{1,0:T(8,128)(2,1)} %param.13, bf16[1,4,8,128]{3,2,1,0:T(8,128)(2,1)S(1)} %fusion.11), kind=kOutput, calls=%fused_computation.16 | convolution fusion | flops 41963520 | bytes 10534912 | tf_op jit(solution)/shard_map/dot_general | solution.py:38
  20.6 1.6 copy.22
  22.2 0.0 reduce-scatter.7.cloned.1.call-update
  22.2 0.0 reduce-scatter.9.cloned.1.call-start
  22.3 0.0 copy-done.1
  22.3 1.0 scatter_custom_fusion
  23.3 0.1 compare_and_fusion.3
  23.4 0.1 compare_select_fusion.7
  23.5 0.6 gather_fusion.4
  24.1 0.6 gather_fusion.3
  24.7 0.7 gather_fusion.6
  25.4 0.6 gather_fusion.1
  26.0 0.6 gather_fusion
  26.6 0.1 reshape.304
  26.7 0.2 reduce_window_sum.18
  26.8 0.1 sub.60
  26.9 0.0 copy-done
  27.0 0.6 gather_fusion.9
  27.6 0.6 gather_fusion.10
  28.2 0.1 compare_and_fusion.2
  28.3 0.1 fusion.31
  28.4 45.4 %all_gather.10 = bf16[2,64,128]{2,0,1:T(2,128)(2,1)S(1)} all-gather(bf16[2,2,128]{2,0,1:T(2,128)(2,1)S(1)} %fusion.31), channel_id=1, replica_groups=mesh['inst'=32,'tp'=8] {'inst'}, dimensions={1}, use_global_device_ids=true | all-gather | bytes 33792 | tf_op jit(solution)/shard_map/all_gather | solution.py:83
  73.8 0.1 select_add_fusion.1
  73.9 0.1 iota_compare_fusion.1
  74.0 0.1 broadcast_select_fusion.1
  74.1 47.1 %all_gather.9 = bf16[1,64,1024]{2,0,1:T(2,128)(2,1)S(1)} all-gather(bf16[1,2,1024]{2,0,1:T(2,128)(2,1)S(1)} %copy.19), channel_id=1, replica_groups=mesh['inst'=32,'tp'=8] {'inst'}, dimensions={1}, use_global_device_ids=true | all-gather | bytes 135168 | tf_op jit(solution)/shard_map/all_gather | solution.py:82
  121.2 0.6 gather_fusion.5
  121.8 0.6 gather_fusion.2
  122.4 0.1 fusion.29
  122.5 34.2 %all-gather.2.cloned.1.call-done = bf16[2,64,512,128]{3,2,0,1:T(8,128)(2,1)} async-done(((bf16[2,2,512,128]{3,2,0,1:T(8,128)(2,1)}), bf16[2,64,512,128]{3,2,0,1:T(8,128)(2,1)}) %all-gather.2.cloned.1.call-update) | async-done | bytes 16777232 | tf_op jit(solution)/shard_map/all_gather | solution.py:81
  156.6 6.5 %gather_fusion.8 = bf16[4,2,512,128]{3,2,1,0:T(8,128)(2,1)S(1)} fusion(bf16[2,64,512,128]{3,2,0,1:T(8,128)(2,1)} %all-gather.2.cloned.1.call-done, s32[1024]{0:T(1024)S(1)} %pad_clamp_fusion), kind=kCustom, calls=%fused_computation.10 | custom fusion | bytes 2097168 | tf_op jit(solution)/shard_map/jit(_take)/gather | solution.py:98
  163.1 0.5 bitcast_select_fusion
  163.6 0.4 fusion.41
  164.1 0.3 fusion.12
  164.3 5.5 %fusion.3 = bf16[5120,4]{0,1:T(4,128)(2,1)S(1)} fusion(bf16[1024,5120]{1,0:T(8,128)(2,1)} %param.13, bf16[1,4,8,128]{3,2,1,0:T(8,128)(2,1)S(1)} %fusion.12), kind=kOutput, calls=%fused_computation.17 | convolution fusion | flops 41963520 | bytes 10534912 | tf_op jit(solution)/shard_map/dot_general | solution.py:38
  169.8 1.6 copy.24
  171.4 0.0 reduce-scatter.9.cloned.1.call-update
  171.4 0.0 reduce-scatter.7.cloned.1.call-done
  171.4 1.6 copy.23
  173.0 1.0 copy.21
  174.1 31.2 %reduce-scatter.9.cloned.1.call-done = bf16[640,4]{1,0:T(8,128)(2,1)} async-done(((bf16[5120,4]{1,0:T(8,128)(2,1)}), bf16[640,4]{1,0:T(8,128)(2,1)}) %reduce-scatter.9.cloned.1.call-update) | async-done | bytes 5136
  205.3 1.6 copy.25
  (14 shorter events, 0.1 us)
Async XLA Ops:
  8.0 148.6 %all-gather.2.cloned.1.call-start = ((), (), s32[]{:S(2)}) async-start(), calls=%async_computation.2 | async-start | bytes 17301504 | tf_op jit(solution)/shard_map/all_gather | solution.py:81
  13.7 8.6 %copy-start.1 = (s32[128]{0:T(128)S(1)}, s32[128]{0:T(128)}, u32[]{:S(2)}) copy-start(s32[128]{0:T(128)} %param.12) | copy-start | bytes 1540
  13.7 157.7 %reduce-scatter.7.cloned.1.call-start = ((), (), s32[]{:S(2)}) async-start(), calls=%async_computation.3 | async-start | bytes 1474560
  15.2 11.8 %copy-start = (s32[128]{0:T(128)S(1)}, s32[128]{0:T(128)}, u32[]{:S(2)}) copy-start(s32[128]{0:T(128)} %param.11) | copy-start | bytes 1540
  22.2 183.0 %reduce-scatter.9.cloned.1.call-start = ((), (), s32[]{:S(2)}) async-start(), calls=%async_computation.4 | async-start | bytes 1474560
Sparse Core Ops, SparseCore 0:
  13.9 142.7 all-gather.1
Sparse Core Ops, SparseCore 1:
  22.3 38.3 reduce-scatter.6
  171.5 33.8 reduce-scatter.8
where the time goes:
time: 215 us; the launch traced here: 214 us
  blocking collectives  92.5 us (43%)
  waiting for transfers between devices  65.4 us (30%)
  local copies, waits for them, and re-layouts  23.4 us (11%)
  between operations  15.6 us (7%)
  matrix products  12.3 us (6%)
  other arithmetic  4.87 us (2%)
    all_gather x1, blocking collectives, on_device(): lax.all_gather(send_query, 'inst', axis=1, tiled=True)  47.1 us
    all_gather x1, blocking collectives, on_device(): lax.all_gather(send_new, 'inst', axis=1, tiled=True)  45.4 us
    all_gather x1, waiting for transfers between devices, on_device(): lax.all_gather(send_caches, 'inst', axis=1, tiled=True)  34.2 us
    unnamed x5, waiting for transfers between devices  31.3 us
    dot_general x2, matrix products, head_term(): lax.dot_general(output_weight, attended, (((0,), (1,)), ((), ())), prefer...  10.9 us
    gather x3, local copies, waits for them, and re-layouts, on_device(): jnp.take(member_remote, remote_index, axis=1)  7.66 us
    unnamed x11, local copies, waits for them, and re-layouts  7.48 us
  transfers between devices with their start and end apart: 3, of which 2 were waited for; matrix products, arithmetic and copies ran while one was open for 16% of the time, Pallas kernels for 0%

commit v1 on v0

v1 whole, which is shorter than its diff:
```python
import functools

import jax
import jax.numpy as jnp
from jax import lax
from jax.experimental import pallas as pl
from jax.experimental.pallas import tpu as pltpu
from jax.sharding import PartitionSpec as P

HD = 128
REQS = 4
CAP = 512
TILE = 16


def bcast_rows(row, rows):
    return jnp.broadcast_to(row, (rows, row.shape[-1]))


def write_row(ref, lead, position, row):
    base = pl.multiple_of((position // TILE) * TILE, TILE)
    window = ref[lead + (pl.ds(base, TILE), slice(None))]
    at = lax.broadcasted_iota(jnp.int32, window.shape, 0) == position - base
    ref[lead + (pl.ds(base, TILE), slice(None))] = jnp.where(at, bcast_rows(row, TILE), window)


def pick_row(rows, slot):
    at = lax.broadcasted_iota(jnp.int32, rows.shape, 0) == slot
    return jnp.sum(jnp.where(at, rows.astype(jnp.float32), 0.0), axis=0, keepdims=True).astype(rows.dtype)


def find_leaver(targets_ref, source_inst, target_inst):
    slot = jnp.int32(0)
    place = jnp.int32(0)
    for j in range(REQS):
        t = targets_ref[source_inst * REQS + j]
        hit = t // REQS == target_inst
        slot = jnp.where(hit, j, slot)
        place = jnp.where(hit, t % REQS, place)
    return slot, place


def prep_kernel(shifts, groups, targets_ref, lengths_ref, new_ref, caches_ref, *rest):
    outs, sems = rest[:-1], rest[-1]
    me = lax.axis_index("inst")
    slots = []
    for n, shift in enumerate(shifts):
        slot, _ = find_leaver(targets_ref, me, lax.rem(me + shift, groups))
        slots.append(slot)
        for kv in range(2):
            pltpu.make_async_copy(caches_ref.at[kv, slot], outs[n].at[kv], sems.at[n, kv]).start()
    for n, shift in enumerate(shifts):
        slot = slots[n]
        length = lengths_ref[me * REQS + slot]
        for kv in range(2):
            pltpu.make_async_copy(caches_ref.at[kv, slot], outs[n].at[kv], sems.at[n, kv]).wait()
            for step in range(2):
                write_row(outs[n], (kv,), length + step, pick_row(new_ref[step, kv], slot))


def attend_kernel(shifts, groups, targets_ref, lengths_ref, queries_ref, new_ref, caches_ref,
                  att_ref, after_ref, *rest):
    pays = rest[: len(shifts)]
    stored, att, in_sems, out_sems = rest[len(shifts):]
    me = lax.axis_index("inst")

    def load(s, kv):
        return pltpu.make_async_copy(caches_ref.at[kv, s], stored.at[kv, s], in_sems.at[kv, s])

    def save(s, kv):
        return pltpu.make_async_copy(stored.at[kv, s], after_ref.at[kv, s], out_sems.at[kv, s])

    for s in range(REQS):
        for kv in range(2):
            load(s, kv).start()
    for s in range(REQS):
        length = lengths_ref[me * REQS + s]
        for kv in range(2):
            load(s, kv).wait()
            for step in range(2):
                write_row(stored, (kv, s), length + step, new_ref[step, kv, s:s + 1, :])
            save(s, kv).start()
        query = jnp.concatenate(
            [queries_ref[0, s], queries_ref[1, s]], axis=0
        )
        scores = lax.dot_general(
            query, stored[0, s], (((1,), (1,)), ((), ())), preferred_element_type=jnp.float32
        ) * HD ** (-0.5)
        live = length + (lax.broadcasted_iota(jnp.int32, scores.shape, 0) >= 8).astype(jnp.int32)
        visible = lax.broadcasted_iota(jnp.int32, scores.shape, 1) <= live
        scores = jnp.where(visible, scores, -jnp.inf)
        weights = jnp.exp(scores - jnp.max(scores, axis=-1, keepdims=True))
        weights = weights / jnp.sum(weights, axis=-1, keepdims=True)
        out = jnp.dot(weights.astype(jnp.bfloat16), stored[1, s], preferred_element_type=jnp.float32)
        out = out.astype(jnp.bfloat16).astype(jnp.float32)
        att[pl.ds(s * 8, 8), :] = out[:8]
        att[pl.ds((REQS + s) * 8, 8), :] = out[8:]
    att_ref[...] = att[...]
    for n, shift in enumerate(shifts):
        slot, _ = find_leaver(targets_ref, me, lax.rem(me + shift, groups))
        row = att[pl.ds(pl.multiple_of((REQS + slot) * 8, 8), 8), :]
        pays[n][...] = jnp.concatenate([row, row], axis=0).astype(jnp.bfloat16)
    for s in range(REQS):
        for kv in range(2):
            save(s, kv).wait()


def project_kernel(shifts, groups, parts, targets_ref, att_ref, *rest):
    pays = rest[: len(shifts)]
    weight_ref, out_ref, att, lhs, weight, sems = rest[len(shifts):]
    me = lax.axis_index("inst")
    width = out_ref.shape[-1]

    def load(p):
        cols = pl.ds(p * width, width)
        return pltpu.make_async_copy(weight_ref.at[:, cols], weight.at[:, cols], sems.at[p])

    for p in range(parts):
        load(p).start()
    att[...] = att_ref[...]
    for n, shift in enumerate(shifts):
        _, place = find_leaver(targets_ref, lax.rem(me + groups - shift, groups), me)
        att[pl.ds(pl.multiple_of((REQS + place) * 8, 8), 8), :] = pays[n][...].astype(jnp.float32)[:8]
    for h in range(8):
        lhs[:, h * HD:(h + 1) * HD] = att[pl.ds(h, 2 * REQS, stride=8), :].astype(jnp.bfloat16)
    for p in range(parts):
        load(p).wait()
        out_ref[p] = jnp.dot(
            lhs[...], weight[:, p * width:(p + 1) * width], preferred_element_type=jnp.float32
        ).astype(jnp.bfloat16)


def finish_kernel(shifts, groups, targets_ref, parts_ref, *rest):
    moved = rest[: len(shifts)]
    _, one_ref, two_ref, after_ref, sems = rest[len(shifts):]
    me = lax.axis_index("inst")
    copies = []
    for n, shift in enumerate(shifts):
        _, place = find_leaver(targets_ref, lax.rem(me + groups - shift, groups), me)
        copies.append(pltpu.make_async_copy(moved[n], after_ref.at[:, place], sems.at[n]))
        copies[-1].start()
    total = jnp.sum(parts_ref[...].astype(jnp.float32), axis=0)
    one_ref[...] = total[:REQS].astype(jnp.bfloat16)
    two_ref[...] = total[REQS:].astype(jnp.bfloat16)
    for copy in copies:
        copy.wait()


VM = pl.BlockSpec(memory_space=pltpu.VMEM)
SM = pl.BlockSpec(memory_space=pltpu.SMEM)
ANY = pl.BlockSpec(memory_space=pl.ANY)
BF = jnp.bfloat16


def shape(dims, kind=BF):
    return jax.ShapeDtypeStruct(dims, kind)


def on_device(caches, queries, new_entries, lengths, targets, output_weight):
    groups = lax.axis_size("inst")
    parts = lax.axis_size("tp")
    shifts = (groups // 2, 1)
    width = output_weight.shape[1] // parts
    perms = [[(i, (i + s) % groups) for i in range(groups)] for s in shifts]

    sent = pl.pallas_call(
        functools.partial(prep_kernel, shifts, groups),
        out_shape=[shape((2, CAP, HD))] * 2,
        in_specs=[SM, SM, VM, ANY],
        out_specs=[VM, VM],
        scratch_shapes=[pltpu.SemaphoreType.DMA((2, 2))],
        name="prep",
    )(targets, lengths, new_entries, caches)
    moved = [lax.ppermute(x, "inst", perm) for x, perm in zip(sent, perms)]

    heads = queries.reshape(2, REQS, 8, HD)
    att, after, *pays = pl.pallas_call(
        functools.partial(attend_kernel, shifts, groups),
        out_shape=[shape((64, HD), jnp.float32), shape(caches.shape)] + [shape((16, HD))] * 2,
        in_specs=[SM, SM, VM, VM, ANY],
        out_specs=[VM, ANY, VM, VM],
        scratch_shapes=[
            pltpu.VMEM(caches.shape, BF),
            pltpu.VMEM((64, HD), jnp.float32),
            pltpu.SemaphoreType.DMA((2, REQS)),
            pltpu.SemaphoreType.DMA((2, REQS)),
        ],
        name="attend",
    )(targets, lengths, heads, new_entries, caches)
    pays = [lax.ppermute(x, "inst", perm) for x, perm in zip(pays, perms)]

    partial = pl.pallas_call(
        functools.partial(project_kernel, shifts, groups, parts),
        out_shape=shape((parts, 2 * REQS, width)),
        in_specs=[SM, VM, VM, VM, ANY],
        out_specs=VM,
        scratch_shapes=[
            pltpu.VMEM((64, HD), jnp.float32),
            pltpu.VMEM((2 * REQS, 8 * HD), BF),
            pltpu.VMEM(output_weight.shape, BF),
            pltpu.SemaphoreType.DMA((parts,)),
        ],
        compiler_params=pltpu.CompilerParams(vmem_limit_bytes=24 << 20),
        name="project",
    )(targets, att, *pays, output_weight)
    shares = lax.all_to_all(partial, "tp", 0, 0)

    one, two, after = pl.pallas_call(
        functools.partial(finish_kernel, shifts, groups),
        out_shape=[shape((REQS, width)), shape((REQS, width)), shape(caches.shape)],
        in_specs=[SM, VM, ANY, ANY, ANY],
        out_specs=[VM, VM, ANY],
        input_output_aliases={4: 2},
        scratch_shapes=[pltpu.SemaphoreType.DMA((2,))],
        name="finish",
    )(targets, shares, *moved, after)
    return one, two, after


def solution(mesh):
    placed = (
        P(None, "inst", None, "tp"),
        P(None, "inst", "tp"),
        P(None, None, "inst", "tp"),
        P(),
        P(),
        P("tp", None),
    )
    return jax.shard_map(
        on_device,
        mesh=mesh,
        in_specs=placed,
        out_specs=(P("inst", "tp"), P("inst", "tp"), P(None, "inst", None, "tp")),
        check_vma=False,
    )
```

time: 215 us -> 70.8 us (0.33)
  the two profiles are of different devices: /device:TPU:24 before, /device:TPU:1 now
where the time goes in v1:
time: 70.8 us; the launch traced here: 70.3 us
  Pallas kernels  30.4 us (43%)
  waiting for transfers between devices  11.5 us (16%)
  starting transfers between devices  10.6 us (15%)
  blocking collectives  9.61 us (14%)
  local copies, waits for them, and re-layouts  7.5 us (11%)
    pallas_call x1, Pallas kernels, on_device(): pl.pallas_call(functools.partial(finish_kernel, shifts, groups), out_shap...  18.5 us
    ppermute x2, waiting for transfers between devices, on_device(): pays = [lax.ppermute(x, 'inst', perm) for x, perm in zip(pays, perms)]  11.5 us
    all_to_all x1, blocking collectives, on_device(): shares = lax.all_to_all(partial, 'tp', 0, 0)  9.61 us
    ppermute x2, starting transfers between devices, on_device(): moved = [lax.ppermute(x, 'inst', perm) for x, perm in zip(sent, perms)]  9.12 us
    unnamed x10, local copies, waits for them, and re-layouts  6.17 us
    pallas_call x1, Pallas kernels, on_device(): pl.pallas_call(functools.partial(project_kernel, shifts, groups, parts),...  4.68 us
    pallas_call x1, Pallas kernels, on_device(): pl.pallas_call(functools.partial(attend_kernel, shifts, groups), out_shap...  4.57 us
    pallas_call x1, Pallas kernels, on_device(): pl.pallas_call(functools.partial(prep_kernel, shifts, groups), out_shape=...  2.66 us
  transfers between devices with their start and end apart: 4, of which 2 were waited for; matrix products, arithmetic and copies ran while one was open for 2% of the time, Pallas kernels for 13%

profile of v1, /device:TPU:1, one launch (start us, length us, event | category | flops | bytes accessed | tf_op | source)
XLA Modules:
  0.0 70.3 jit_solution(14630362091462031460)
XLA Ops:
  0.6 2.7 %prep.1 = (bf16[2,512,128]{2,1,0:T(8,128)(2,1)}, bf16[2,512,128]{2,1,0:T(8,128)(2,1)}) custom-call(s32[128]{0:T(128)} %targets_ref.7, s32[128]{0:T(128)} %lengths_ref.3, bf16[2,2,4,128]{3,2,1,0:T(4,128)(2,1)} %new_ref.3, bf16[2,4,512,128]{3,2,1,0:T(8,128)(2,1)} %caches_ref.3), custom_call_target="tpu_custom_call" | custom-call | tf_op jit(solution)/shard_map/prep/pallas_call | solution.py:166
  3.3 7.8 %collective-permute-start.2 = (bf16[2,512,128]{2,1,0:T(8,128)(2,1)}, bf16[2,512,128]{2,1,0:T(8,128)(2,1)S(1)}, u32[]{:S(2)}, u32[]{:S(2)}) collective-permute-start(bf16[2,512,128]{2,1,0:T(8,128)(2,1)} %get-tuple-element.12), channel_id=1, source_target_pairs={{0,128},{8,136},{16,144},{24,152},{32,160},{40,168},{48,176},{56,1... | collective-permute-start | bytes 786440 | tf_op jit(solution)/shard_map/ppermute | solution.py:174
  11.1 1.3 %collective-permute-start.3 = (bf16[2,512,128]{2,1,0:T(8,128)(2,1)}, bf16[2,512,128]{2,1,0:T(8,128)(2,1)S(1)}, u32[]{:S(2)}, u32[]{:S(2)}) collective-permute-start(bf16[2,512,128]{2,1,0:T(8,128)(2,1)} %get-tuple-element.13), channel_id=1, source_target_pairs={{0,8},{8,16},{16,24},{24,32},{32,40},{40,48},{48,56},{56,64},{64,7... | collective-permute-start | bytes 786440 | tf_op jit(solution)/shard_map/ppermute | solution.py:174
  12.4 1.3 %reshape.9.queries_ref = bf16[2,4,8,128]{3,2,1,0:T(8,128)(2,1)} reshape(bf16[2,4,1024]{2,1,0:T(4,128)(2,1)} %param.7) | data formatting | bytes 32768 | tf_op jit(solution)/shard_map/reshape | solution.py:176
  13.7 4.6 %attend.1 = (f32[64,128]{1,0:T(8,128)}, bf16[2,4,512,128]{3,2,1,0:T(8,128)(2,1)}, bf16[16,128]{1,0:T(8,128)(2,1)}, bf16[16,128]{1,0:T(8,128)(2,1)}) custom-call(s32[128]{0:T(128)} %targets_ref.7, s32[128]{0:T(128)} %lengths_ref.3, bf16[2,4,8,128]{3,2,1,0:T(8,128)(2,1)} %reshape.9.queries_ref, bf16[2,2,4,128]{3,2,1,0:T(4,128)(2,1)} %new_ref.3, ...), custom_call_target="tpu_custom_call" | custom-call | tf_op jit(solution)/shard_map/attend/pallas_call | solution.py:177
  18.3 0.2 collective-permute-start
  18.5 1.3 %collective-permute-start.1 = (bf16[16,128]{1,0:T(8,128)(2,1)}, bf16[16,128]{1,0:T(8,128)(2,1)S(1)}, u32[]{:S(2)}, u32[]{:S(2)}) collective-permute-start(bf16[16,128]{1,0:T(8,128)(2,1)} %get-tuple-element.11), channel_id=1, source_target_pairs={{0,8},{8,16},{16,24},{24,32},{32,40},{40,48},{48,56},{56,64},{64,7... | collective-permute-start | bytes 12296 | tf_op jit(solution)/shard_map/ppermute | solution.py:190
  19.8 5.6 %collective-permute-done.rest_0_ = bf16[16,128]{1,0:T(8,128)(2,1)S(1)} collective-permute-done((bf16[16,128]{1,0:T(8,128)(2,1)}, bf16[16,128]{1,0:T(8,128)(2,1)S(1)}, u32[]{:S(2)}, u32[]{:S(2)}) %collective-permute-start) | collective-permute-done | bytes 4128 | tf_op jit(solution)/shard_map/ppermute | solution.py:190
  25.4 5.9 %collective-permute-done.1.rest_1_ = bf16[16,128]{1,0:T(8,128)(2,1)S(1)} collective-permute-done((bf16[16,128]{1,0:T(8,128)(2,1)}, bf16[16,128]{1,0:T(8,128)(2,1)S(1)}, u32[]{:S(2)}, u32[]{:S(2)}) %collective-permute-start.1) | collective-permute-done | bytes 4128 | tf_op jit(solution)/shard_map/ppermute | solution.py:190
  31.3 0.0 copy-start
  31.3 4.0 %copy-done = bf16[1024,5120]{1,0:T(8,128)(2,1)S(1)} copy-done((bf16[1024,5120]{1,0:T(8,128)(2,1)S(1)}, bf16[1024,5120]{1,0:T(8,128)(2,1)}, u32[]{:S(2)}) %copy-start) | copy-done | bytes 10485784
  35.3 0.0 copy-start.1
  35.3 0.8 %copy-done.1 = f32[64,128]{1,0:T(8,128)S(1)} copy-done((f32[64,128]{1,0:T(8,128)S(1)}, f32[64,128]{1,0:T(8,128)}, u32[]{:S(2)}) %copy-start.1) | copy-done | bytes 32792
  36.1 0.0 copy-start.2
  36.1 0.7 copy-done.2
  36.7 4.7 %project.1 = bf16[8,8,640]{2,1,0:T(8,128)(2,1)S(1)} custom-call(s32[128]{0:T(128)S(1)} %copy-done.2, f32[64,128]{1,0:T(8,128)S(1)} %copy-done.1, bf16[16,128]{1,0:T(8,128)(2,1)S(1)} %collective-permute-done.rest_0_, bf16[16,128]{1,0:T(8,128)(2,1)S(1)} %collective-permute-done.1.rest_1_, bf16[1024,5120]{1,0:T(8,128)(2,1)S(1)} %copy-done), custom_call_target="tpu_custom_call" | custom-call | tf_op jit(solution)/shard_map/project/pallas_call | solution.py:192
  41.4 9.6 %all_to_all.5.parts_ref = bf16[8,8,640]{2,1,0:T(8,128)(2,1)} all-to-all(bf16[8,8,640]{2,1,0:T(8,128)(2,1)S(1)} %project.1), channel_id=1, replica_groups=mesh['inst'=32,'tp'=8] {'tp'}, dimensions={0} | all-to-all | bytes 163840 | tf_op jit(solution)/shard_map/all_to_all | solution.py:206
  51.0 0.0 collective-permute-done.2.rest_0_
  51.0 0.0 copy-start.3
  51.0 0.0 collective-permute-done.3.rest_1_
  51.0 0.0 copy-start.4
  51.0 0.7 copy-done.3
  51.7 0.1 copy-done.4
  51.8 18.5 %finish.1 = (bf16[4,640]{1,0:T(4,128)(2,1)}, bf16[4,640]{1,0:T(4,128)(2,1)}, bf16[2,4,512,128]{3,2,1,0:T(8,128)(2,1)}) custom-call(s32[128]{0:T(128)} %targets_ref.7, bf16[8,8,640]{2,1,0:T(8,128)(2,1)} %all_to_all.5.parts_ref, bf16[2,512,128]{2,1,0:T(8,128)(2,1)} %copy-done.3, bf16[2,512,128]{2,1,0:T(8,128)(2,1)} %copy-done.4, ...), custom_call_target="tpu_custom_call", output_to_operand_aliasing={{2}: (4, {})} | custom-call | tf_op jit(solution)/shard_map/finish/pallas_call | solution.py:208
Async XLA Ops:
  3.3 47.7 %collective-permute-start.2 = (bf16[2,512,128]{2,1,0:T(8,128)(2,1)}, bf16[2,512,128]{2,1,0:T(8,128)(2,1)S(1)}, u32[]{:S(2)}, u32[]{:S(2)}) collective-permute-start(bf16[2,512,128]{2,1,0:T(8,128)(2,1)} %get-tuple-element.12), channel_id=1, source_target_pairs={{0,128},{8,136},{16,144},{24,152},{32,160},{40,168},{48,176},{56,1... | collective-permute-start | bytes 786440 | tf_op jit(solution)/shard_map/ppermute | solution.py:174
  11.1 39.9 %collective-permute-start.3 = (bf16[2,512,128]{2,1,0:T(8,128)(2,1)}, bf16[2,512,128]{2,1,0:T(8,128)(2,1)S(1)}, u32[]{:S(2)}, u32[]{:S(2)}) collective-permute-start(bf16[2,512,128]{2,1,0:T(8,128)(2,1)} %get-tuple-element.13), channel_id=1, source_target_pairs={{0,8},{8,16},{16,24},{24,32},{32,40},{40,48},{48,56},{56,64},{64,7... | collective-permute-start | bytes 786440 | tf_op jit(solution)/shard_map/ppermute | solution.py:174
  18.3 7.1 %collective-permute-start = (bf16[16,128]{1,0:T(8,128)(2,1)}, bf16[16,128]{1,0:T(8,128)(2,1)S(1)}, u32[]{:S(2)}, u32[]{:S(2)}) collective-permute-start(bf16[16,128]{1,0:T(8,128)(2,1)} %get-tuple-element.10), channel_id=1, source_target_pairs={{0,128},{8,136},{16,144},{24,152},{32,160},{40,168},{48,176},{56,1... | collective-permute-start | bytes 12296 | tf_op jit(solution)/shard_map/ppermute | solution.py:190
  18.5 12.8 %collective-permute-start.1 = (bf16[16,128]{1,0:T(8,128)(2,1)}, bf16[16,128]{1,0:T(8,128)(2,1)S(1)}, u32[]{:S(2)}, u32[]{:S(2)}) collective-permute-start(bf16[16,128]{1,0:T(8,128)(2,1)} %get-tuple-element.11), channel_id=1, source_target_pairs={{0,8},{8,16},{16,24},{24,32},{32,40},{40,48},{48,56},{56,64},{64,7... | collective-permute-start | bytes 12296 | tf_op jit(solution)/shard_map/ppermute | solution.py:190
  31.3 4.0 %copy-start = (bf16[1024,5120]{1,0:T(8,128)(2,1)S(1)}, bf16[1024,5120]{1,0:T(8,128)(2,1)}, u32[]{:S(2)}) copy-start(bf16[1024,5120]{1,0:T(8,128)(2,1)} %rest_2_.1) | copy-start | bytes 31457284
  35.3 0.8 %copy-start.1 = (f32[64,128]{1,0:T(8,128)S(1)}, f32[64,128]{1,0:T(8,128)}, u32[]{:S(2)}) copy-start(f32[64,128]{1,0:T(8,128)} %get-tuple-element.9.att_ref) | copy-start | bytes 98308
  36.1 0.7 copy-start.2
  51.0 0.7 %copy-start.3 = (bf16[2,512,128]{2,1,0:T(8,128)(2,1)}, bf16[2,512,128]{2,1,0:T(8,128)(2,1)S(1)}, u32[]{:S(2)}) copy-start(bf16[2,512,128]{2,1,0:T(8,128)(2,1)S(1)} %collective-permute-done.2.rest_0_) | copy-start | bytes 786436
  51.0 0.8 %copy-start.4 = (bf16[2,512,128]{2,1,0:T(8,128)(2,1)}, bf16[2,512,128]{2,1,0:T(8,128)(2,1)S(1)}, u32[]{:S(2)}) copy-start(bf16[2,512,128]{2,1,0:T(8,128)(2,1)S(1)} %collective-permute-done.3.rest_1_) | copy-start | bytes 786436

commit v2 on v1

v2 whole, which is shorter than its diff:
```python
import functools

import jax
import jax.numpy as jnp
from jax import lax
from jax.experimental import pallas as pl
from jax.experimental.pallas import tpu as pltpu
from jax.sharding import PartitionSpec as P

HD = 128
REQS = 4
CAP = 512
TILE = 16


def bcast_rows(row, rows):
    return jnp.broadcast_to(row, (rows, row.shape[-1]))


def write_row(ref, lead, position, row):
    base = pl.multiple_of((position // TILE) * TILE, TILE)
    window = ref[lead + (pl.ds(base, TILE), slice(None))]
    at = lax.broadcasted_iota(jnp.int32, window.shape, 0) == position - base
    ref[lead + (pl.ds(base, TILE), slice(None))] = jnp.where(at, bcast_rows(row, TILE), window)


def pick_row(rows, slot):
    at = lax.broadcasted_iota(jnp.int32, rows.shape, 0) == slot
    return jnp.sum(jnp.where(at, rows.astype(jnp.float32), 0.0), axis=0, keepdims=True).astype(rows.dtype)


def find_leaver(targets_ref, source_inst, target_inst):
    slot = jnp.int32(0)
    place = jnp.int32(0)
    for j in range(REQS):
        t = targets_ref[source_inst * REQS + j]
        hit = t // REQS == target_inst
        slot = jnp.where(hit, j, slot)
        place = jnp.where(hit, t % REQS, place)
    return slot, place


def step_two_rows(targets_ref, me, shifts, groups):
    rows = []
    rank = jnp.int32(REQS)
    for j in range(REQS):
        inst = targets_ref[me * REQS + j] // REQS
        row = rank
        for n, shift in enumerate(shifts):
            row = jnp.where(inst == lax.rem(me + shift, groups), 2 * REQS - len(shifts) + n, row)
        rows.append(row)
        rank = rank + (inst == me).astype(jnp.int32)
    return rows


def start_all(pairs, sems):
    copies = [pltpu.make_async_copy(a, b, sems.at[n]) for n, (a, b) in enumerate(pairs)]
    for copy in copies:
        copy.start()
    return copies


def wait_all(copies):
    for copy in copies:
        copy.wait()


def prep_kernel(shifts, groups, targets_hbm, lengths_hbm, new_hbm, caches_hbm, *rest):
    outs = rest[:len(shifts)]
    targets, lengths, new, stored, small_sems, sems = rest[len(shifts):]
    me = lax.axis_index("inst")
    smalls = start_all([(targets_hbm, targets), (lengths_hbm, lengths), (new_hbm, new)], small_sems)
    bigs = start_all([(caches_hbm.at[:, s], stored.at[:, s]) for s in range(REQS)], sems)
    wait_all(smalls)
    wait_all(bigs)
    for n, shift in enumerate(shifts):
        slot, _ = find_leaver(targets, me, lax.rem(me + shift, groups))
        length = lengths[me * REQS + slot]
        for kv in range(2):
            outs[n][kv] = stored[kv, slot]
            for step in range(2):
                write_row(outs[n], (kv,), length + step, pick_row(new[step, kv], slot))


def step_kernel(shifts, groups, parts, targets_hbm, lengths_hbm, queries_hbm, new_hbm, caches_ref, weight_ref,
                out_ref, after_ref, targets_ref, lengths_ref, queries_ref, new_ref, stored, weight, query,
                att, lhs, small_sems, in_sems, out_sems, w_sems):
    me = lax.axis_index("inst")
    width = out_ref.shape[-1]

    def load(s, kv):
        return pltpu.make_async_copy(caches_ref.at[kv, s], stored.at[kv, s], in_sems.at[kv, s])

    def save(s, kv):
        return pltpu.make_async_copy(stored.at[kv, s], after_ref.at[kv, s], out_sems.at[kv, s])

    def load_weight(p):
        cols = pl.ds(p * width, width)
        return pltpu.make_async_copy(weight_ref.at[:, cols], weight.at[:, cols], w_sems.at[p])

    smalls = start_all(
        [(queries_hbm, queries_ref), (new_hbm, new_ref), (lengths_hbm, lengths_ref), (targets_hbm, targets_ref)],
        small_sems,
    )
    for kv in range(2):
        for s in range(REQS):
            load(s, kv).start()
    for p in range(parts):
        load_weight(p).start()
    wait_all(smalls)
    for step in range(2):
        for h in range(8):
            rows = queries_ref[step, :, h * HD:(h + 1) * HD].astype(jnp.float32)
            query[pl.ds(step * 8 + h, REQS, stride=16), :] = rows
    for kv in range(2):
        for s in range(REQS):
            load(s, kv).wait()
            for step in range(2):
                write_row(stored, (kv, s), lengths_ref[me * REQS + s] + step, new_ref[step, kv, s:s + 1, :])
            save(s, kv).start()
    probs = []
    for s in range(REQS):
        scores = lax.dot_general(
            query[s * 16:(s + 1) * 16, :].astype(BF), stored[0, s], (((1,), (1,)), ((), ())),
            preferred_element_type=jnp.float32,
        ) * HD ** (-0.5)
        live = lengths_ref[me * REQS + s] + (
            lax.broadcasted_iota(jnp.int32, scores.shape, 0) >= 8
        ).astype(jnp.int32)
        visible = lax.broadcasted_iota(jnp.int32, scores.shape, 1) <= live
        scores = jnp.where(visible, scores, -jnp.inf)
        weights = jnp.exp(scores - jnp.max(scores, axis=-1, keepdims=True))
        probs.append((weights / jnp.sum(weights, axis=-1, keepdims=True)).astype(BF))
    rows_two = step_two_rows(targets_ref, me, shifts, groups)
    for s in range(REQS):
        out = jnp.dot(probs[s], stored[1, s], preferred_element_type=jnp.float32)
        att[pl.ds(s * 8, 8), :] = out[:8]
        att[pl.ds(pl.multiple_of(rows_two[s] * 8, 8), 8), :] = out[8:]
    for h in range(8):
        lhs[:, h * HD:(h + 1) * HD] = att[pl.ds(h, 2 * REQS, stride=8), :].astype(BF)
    for p in range(parts):
        load_weight(p).wait()
        out_ref[p] = jnp.dot(
            lhs[...], weight[:, p * width:(p + 1) * width], preferred_element_type=jnp.float32
        ).astype(BF)
    for kv in range(2):
        for s in range(REQS):
            save(s, kv).wait()


def sum_kernel(shares_ref, one_ref, stay_ref, *pays):
    total = jnp.sum(shares_ref[...].astype(jnp.float32), axis=0)
    one_ref[...] = total[:REQS].astype(BF)
    stay_ref[...] = total
    for n, pay in enumerate(pays):
        row = 2 * REQS - len(pays) + n
        pay[...] = bcast_rows(total[row:row + 1], pay.shape[0]).astype(BF)


def finish_kernel(shifts, groups, targets_hbm, stay_ref, *rest):
    many = len(shifts)
    pays, moved = rest[:many], rest[many:2 * many]
    _, two_ref, after_ref, targets_ref, sem, sems = rest[2 * many:]
    me = lax.axis_index("inst")
    copy = pltpu.make_async_copy(targets_hbm, targets_ref, sem)
    copy.start()
    copy.wait()
    places = []
    copies = []
    for n, shift in enumerate(shifts):
        _, place = find_leaver(targets_ref, lax.rem(me + groups - shift, groups), me)
        places.append(place)
        copies.append(pltpu.make_async_copy(moved[n], after_ref.at[:, place], sems.at[n]))
        copies[-1].start()
    rows_two = step_two_rows(targets_ref, me, shifts, groups)
    at = lax.broadcasted_iota(jnp.int32, two_ref.shape, 0)
    out = jnp.zeros(two_ref.shape, jnp.float32)
    for r in range(REQS, 2 * REQS - many):
        for s in range(REQS):
            out = jnp.where(
                (at == s) & (rows_two[s] == r), bcast_rows(stay_ref[r:r + 1, :], REQS), out
            )
    for n in range(many):
        row = pays[n][...].astype(jnp.float32)[:1]
        out = jnp.where(at == places[n], bcast_rows(row, REQS), out)
    two_ref[...] = out.astype(BF)
    for copy in copies:
        copy.wait()


VM = pl.BlockSpec(memory_space=pltpu.VMEM)
BF = jnp.bfloat16


def shape(dims, kind=BF):
    return jax.ShapeDtypeStruct(dims, kind)
HBM = pl.BlockSpec(memory_space=pltpu.HBM)


def limit(mib):
    return pltpu.CompilerParams(vmem_limit_bytes=mib << 20)


def on_device(caches, queries, new_entries, lengths, targets, output_weight):
    groups = lax.axis_size("inst")
    parts = lax.axis_size("tp")
    shifts = (groups // 2, 1)
    many = len(shifts)
    width = output_weight.shape[1] // parts
    perms = [[(i, (i + s) % groups) for i in range(groups)] for s in shifts]

    caches, queries, new_entries, lengths, targets, output_weight = [
        pltpu.with_memory_space_constraint(x, pltpu.HBM)
        for x in (caches, queries, new_entries, lengths, targets, output_weight)
    ]
    smem = pltpu.SMEM(targets.shape, jnp.int32)
    sent = pl.pallas_call(
        functools.partial(prep_kernel, shifts, groups),
        out_shape=[shape((2, CAP, HD))] * many,
        in_specs=[HBM] * 4,
        out_specs=[VM] * many,
        scratch_shapes=[
            smem,
            smem,
            pltpu.VMEM(new_entries.shape, BF),
            pltpu.VMEM(caches.shape, BF),
            pltpu.SemaphoreType.DMA((3,)),
            pltpu.SemaphoreType.DMA((REQS,)),
        ],
        compiler_params=limit(4),
        name="prep",
    )(targets, lengths, new_entries, caches)
    moved = [lax.ppermute(x, "inst", perm) for x, perm in zip(sent, perms)]

    partial, after = pl.pallas_call(
        functools.partial(step_kernel, shifts, groups, parts),
        out_shape=[shape((parts, 2 * REQS, width)), shape(caches.shape)],
        in_specs=[HBM] * 6,
        out_specs=[VM, HBM],
        scratch_shapes=[
            smem,
            smem,
            pltpu.VMEM(queries.shape, BF),
            pltpu.VMEM(new_entries.shape, BF),
            pltpu.VMEM(caches.shape, BF),
            pltpu.VMEM(output_weight.shape, BF),
            pltpu.VMEM((16 * REQS, HD), jnp.float32),
            pltpu.VMEM((16 * REQS, HD), jnp.float32),
            pltpu.VMEM((2 * REQS, 8 * HD), BF),
            pltpu.SemaphoreType.DMA((4,)),
            pltpu.SemaphoreType.DMA((2, REQS)),
            pltpu.SemaphoreType.DMA((2, REQS)),
            pltpu.SemaphoreType.DMA((parts,)),
        ],
        compiler_params=limit(20),
        name="step",
    )(targets, lengths, queries, new_entries, caches, output_weight)
    shares = lax.all_to_all(partial, "tp", 0, 0)

    one, stay, *pays = pl.pallas_call(
        sum_kernel,
        out_shape=[shape((REQS, width)), shape((2 * REQS, width), jnp.float32)] + [shape((8, width))] * many,
        in_specs=[VM],
        out_specs=[VM] * (2 + many),
        compiler_params=limit(4),
        name="sum",
    )(shares)
    pays = [lax.ppermute(x, "inst", perm) for x, perm in zip(pays, perms)]

    two, after = pl.pallas_call(
        functools.partial(finish_kernel, shifts, groups),
        out_shape=[shape((REQS, width)), shape(caches.shape)],
        in_specs=[HBM, VM] + [VM] * many + [VM] * many + [HBM],
        out_specs=[VM, HBM],
        input_output_aliases={2 + 2 * many: 1},
        scratch_shapes=[smem, pltpu.SemaphoreType.DMA, pltpu.SemaphoreType.DMA((many,))],
        compiler_params=limit(4),
        name="finish",
    )(targets, stay, *pays, *moved, after)
    return one, two, after


def solution(mesh):
    placed = (
        P(None, "inst", None, "tp"),
        P(None, "inst", "tp"),
        P(None, None, "inst", "tp"),
        P(),
        P(),
        P("tp", None),
    )
    return jax.shard_map(
        on_device,
        mesh=mesh,
        in_specs=placed,
        out_specs=(P("inst", "tp"), P("inst", "tp"), P(None, "inst", None, "tp")),
        check_vma=False,
    )
```

time: 70.8 us -> 38.6 us (0.55)
  the two profiles are of different devices: /device:TPU:1 before, /device:TPU:8 now
where the time goes in v2:
time: 38.6 us; the launch traced here: 38.4 us
  Pallas kernels  11.5 us (30%)
  starting transfers between devices  10.2 us (26%)
  blocking collectives  9.81 us (25%)
  waiting for transfers between devices  6.21 us (16%)
  between operations  0.65 us (2%)
    all_to_all x1, blocking collectives, on_device(): shares = lax.all_to_all(partial, 'tp', 0, 0)  9.81 us
    ppermute x2, starting transfers between devices, on_device(): moved = [lax.ppermute(x, 'inst', perm) for x, perm in zip(sent, perms)]  8.85 us
    pallas_call x1, Pallas kernels, on_device(): pl.pallas_call(functools.partial(step_kernel, shifts, groups, parts), out...  7.44 us
    ppermute x2, waiting for transfers between devices, on_device(): pays = [lax.ppermute(x, 'inst', perm) for x, perm in zip(pays, perms)]  6.2 us
    pallas_call x1, Pallas kernels, on_device(): pl.pallas_call(functools.partial(finish_kernel, shifts, groups), out_shap...  2.11 us
    ppermute x2, starting transfers between devices, on_device(): pays = [lax.ppermute(x, 'inst', perm) for x, perm in zip(pays, perms)]  1.38 us
    pallas_call x1, Pallas kernels, on_device(): pl.pallas_call(functools.partial(prep_kernel, shifts, groups), out_shape=...  1.35 us
  transfers between devices with their start and end apart: 4, of which 1 were waited for; matrix products, arithmetic and copies ran while one was open for 0% of the time, Pallas kernels for 21%

profile of v2, /device:TPU:8, one launch (start us, length us, event | category | flops | bytes accessed | tf_op | source)
XLA Modules:
  0.0 38.4 jit_solution(2307714421942922773)
XLA Ops:
  0.6 1.4 %prep.1 = (bf16[2,512,128]{2,1,0:T(8,128)(2,1)S(1)}, bf16[2,512,128]{2,1,0:T(8,128)(2,1)S(1)}) custom-call(s32[128]{0:T(128)} %targets_hbm.5, s32[128]{0:T(128)} %lengths_hbm.3, bf16[2,2,4,128]{3,2,1,0:T(4,128)(2,1)} %new_hbm.3, bf16[2,4,512,128]{3,2,1,0:T(8,128)(2,1)} %caches_hbm.1), custom_call_target="tpu_custom_call" | custom-call | tf_op jit(solution)/shard_map/prep/pallas_call | solution.py:217
  2.0 7.3 %collective-permute-start.2 = (bf16[2,512,128]{2,1,0:T(8,128)(2,1)S(1)}, bf16[2,512,128]{2,1,0:T(8,128)(2,1)S(1)}, u32[]{:S(2)}, u32[]{:S(2)}) collective-permute-start(bf16[2,512,128]{2,1,0:T(8,128)(2,1)S(1)} %get-tuple-element.18), channel_id=1, source_target_pairs={{0,128},{8,136},{16,144},{24,152},{32,160},{40,168},{48,176},{56,1... | collective-permute-start | bytes 786440 | tf_op jit(solution)/shard_map/ppermute | solution.py:233
  9.3 1.6 %collective-permute-start.3 = (bf16[2,512,128]{2,1,0:T(8,128)(2,1)S(1)}, bf16[2,512,128]{2,1,0:T(8,128)(2,1)S(1)}, u32[]{:S(2)}, u32[]{:S(2)}) collective-permute-start(bf16[2,512,128]{2,1,0:T(8,128)(2,1)S(1)} %get-tuple-element.19), channel_id=1, source_target_pairs={{0,8},{8,16},{16,24},{24,32},{32,40},{40,48},{48,56},{56,64},{64,7... | collective-permute-start | bytes 786440 | tf_op jit(solution)/shard_map/ppermute | solution.py:233
  10.8 7.4 %step.1 = (bf16[8,8,640]{2,1,0:T(8,128)(2,1)S(1)}, bf16[2,4,512,128]{3,2,1,0:T(8,128)(2,1)}) custom-call(s32[128]{0:T(128)} %targets_hbm.5, s32[128]{0:T(128)} %lengths_hbm.3, bf16[2,4,1024]{2,1,0:T(4,128)(2,1)} %queries_hbm.1, bf16[2,2,4,128]{3,2,1,0:T(4,128)(2,1)} %new_hbm.3, bf16[2,4,512,128]{3,2,1,0:T(8,128)(2,1)} %caches_hbm.1, ...), custom_call_target="tpu_custom_call" | custom-call | tf_op jit(solution)/shard_map/step/pallas_call | solution.py:235
  18.3 9.8 %all_to_all.5.shares_ref = bf16[8,8,640]{2,1,0:T(8,128)(2,1)S(1)} all-to-all(bf16[8,8,640]{2,1,0:T(8,128)(2,1)S(1)} %get-tuple-element.13), channel_id=1, replica_groups=mesh['inst'=32,'tp'=8] {'tp'}, dimensions={0} | all-to-all | bytes 163840 | tf_op jit(solution)/shard_map/all_to_all | solution.py:258
  28.1 0.6 %sum.1 = (bf16[4,640]{1,0:T(4,128)(2,1)}, f32[8,640]{1,0:T(8,128)S(1)}, bf16[8,640]{1,0:T(8,128)(2,1)S(1)}, bf16[8,640]{1,0:T(8,128)(2,1)S(1)}) custom-call(bf16[8,8,640]{2,1,0:T(8,128)(2,1)S(1)} %all_to_all.5.shares_ref), custom_call_target="tpu_custom_call" | custom-call | tf_op jit(solution)/shard_map/sum/pallas_call | solution.py:260
  28.7 0.1 collective-permute-start
  28.8 1.3 %collective-permute-start.1 = (bf16[8,640]{1,0:T(8,128)(2,1)S(1)}, bf16[8,640]{1,0:T(8,128)(2,1)S(1)}, u32[]{:S(2)}, u32[]{:S(2)}) collective-permute-start(bf16[8,640]{1,0:T(8,128)(2,1)S(1)} %get-tuple-element.17), channel_id=1, source_target_pairs={{0,8},{8,16},{16,24},{24,32},{32,40},{40,48},{48,56},{56,64},{64,7... | collective-permute-start | bytes 30728 | tf_op jit(solution)/shard_map/ppermute | solution.py:268
  30.1 6.2 %collective-permute-done.rest_0_ = bf16[8,640]{1,0:T(8,128)(2,1)S(1)} collective-permute-done((bf16[8,640]{1,0:T(8,128)(2,1)S(1)}, bf16[8,640]{1,0:T(8,128)(2,1)S(1)}, u32[]{:S(2)}, u32[]{:S(2)}) %collective-permute-start) | collective-permute-done | bytes 10272 | tf_op jit(solution)/shard_map/ppermute | solution.py:268
  36.3 0.0 collective-permute-done.1.rest_1_
  36.3 0.0 collective-permute-done.2.rest_2_
  36.3 0.0 collective-permute-done.3.rest_3_
  36.3 2.1 %finish.1 = (bf16[4,640]{1,0:T(4,128)(2,1)}, bf16[2,4,512,128]{3,2,1,0:T(8,128)(2,1)}) custom-call(s32[128]{0:T(128)} %targets_hbm.5, f32[8,640]{1,0:T(8,128)S(1)} %get-tuple-element.15.stay_ref, bf16[8,640]{1,0:T(8,128)(2,1)S(1)} %collective-permute-done.rest_0_, ...), custom_call_target="tpu_custom_call", output_to_operand_aliasing={{1}: (6, {})} | custom-call | tf_op jit(solution)/shard_map/finish/pallas_call | solution.py:270
Async XLA Ops:
  2.0 34.3 %collective-permute-start.2 = (bf16[2,512,128]{2,1,0:T(8,128)(2,1)S(1)}, bf16[2,512,128]{2,1,0:T(8,128)(2,1)S(1)}, u32[]{:S(2)}, u32[]{:S(2)}) collective-permute-start(bf16[2,512,128]{2,1,0:T(8,128)(2,1)S(1)} %get-tuple-element.18), channel_id=1, source_target_pairs={{0,128},{8,136},{16,144},{24,152},{32,160},{40,168},{48,176},{56,1... | collective-permute-start | bytes 786440 | tf_op jit(solution)/shard_map/ppermute | solution.py:233
  9.3 27.0 %collective-permute-start.3 = (bf16[2,512,128]{2,1,0:T(8,128)(2,1)S(1)}, bf16[2,512,128]{2,1,0:T(8,128)(2,1)S(1)}, u32[]{:S(2)}, u32[]{:S(2)}) collective-permute-start(bf16[2,512,128]{2,1,0:T(8,128)(2,1)S(1)} %get-tuple-element.19), channel_id=1, source_target_pairs={{0,8},{8,16},{16,24},{24,32},{32,40},{40,48},{48,56},{56,64},{64,7... | collective-permute-start | bytes 786440 | tf_op jit(solution)/shard_map/ppermute | solution.py:233
  28.7 7.6 %collective-permute-start = (bf16[8,640]{1,0:T(8,128)(2,1)S(1)}, bf16[8,640]{1,0:T(8,128)(2,1)S(1)}, u32[]{:S(2)}, u32[]{:S(2)}) collective-permute-start(bf16[8,640]{1,0:T(8,128)(2,1)S(1)} %get-tuple-element.16), channel_id=1, source_target_pairs={{0,128},{8,136},{16,144},{24,152},{32,160},{40,168},{48,176},{56,1... | collective-permute-start | bytes 30728 | tf_op jit(solution)/shard_map/ppermute | solution.py:268
  28.8 7.5 %collective-permute-start.1 = (bf16[8,640]{1,0:T(8,128)(2,1)S(1)}, bf16[8,640]{1,0:T(8,128)(2,1)S(1)}, u32[]{:S(2)}, u32[]{:S(2)}) collective-permute-start(bf16[8,640]{1,0:T(8,128)(2,1)S(1)} %get-tuple-element.17), channel_id=1, source_target_pairs={{0,8},{8,16},{16,24},{24,32},{32,40},{40,48},{48,56},{56,64},{64,7... | collective-permute-start | bytes 30728 | tf_op jit(solution)/shard_map/ppermute | solution.py:268

commit v3 on v1

v3 whole, which is shorter than its diff:
```python
import functools

import jax
import jax.numpy as jnp
from jax import lax
from jax.experimental import pallas as pl
from jax.experimental.pallas import tpu as pltpu
from jax.sharding import PartitionSpec as P

HD = 128
REQS = 4
CAP = 512
TILE = 16
PAY_ROWS = (16, 256)


def bcast_rows(row, rows):
    return jnp.broadcast_to(row, (rows, row.shape[-1]))


def write_row(ref, lead, position, row):
    base = pl.multiple_of((position // TILE) * TILE, TILE)
    window = ref[lead + (pl.ds(base, TILE), slice(None))]
    at = lax.broadcasted_iota(jnp.int32, window.shape, 0) == position - base
    ref[lead + (pl.ds(base, TILE), slice(None))] = jnp.where(at, bcast_rows(row, TILE), window)


def pick_row(rows, slot):
    at = lax.broadcasted_iota(jnp.int32, rows.shape, 0) == slot
    return jnp.sum(jnp.where(at, rows.astype(jnp.float32), 0.0), axis=0, keepdims=True).astype(rows.dtype)


def find_leaver(targets_ref, source_inst, target_inst):
    slot = jnp.int32(0)
    place = jnp.int32(0)
    for j in range(REQS):
        t = targets_ref[source_inst * REQS + j]
        hit = t // REQS == target_inst
        slot = jnp.where(hit, j, slot)
        place = jnp.where(hit, t % REQS, place)
    return slot, place


def attend_kernel(shifts, groups, targets_hbm, lengths_hbm, queries_hbm, new_hbm, caches_hbm, *rest):
    many = len(shifts)
    whole, halves, pays = rest[0], rest[1:3], rest[3:3 + many]
    (att, after_hbm, targets, lengths, queries, new, stored, query, small_sems, in_sems,
     out_sems) = rest[3 + many:]
    me = lax.axis_index("inst")
    smalls = [
        pltpu.make_async_copy(source, target, small_sems.at[n])
        for n, (source, target) in enumerate(
            [(lengths_hbm, lengths), (new_hbm, new), (targets_hbm, targets), (queries_hbm, queries)]
        )
    ]

    def load(s, kv):
        return pltpu.make_async_copy(caches_hbm.at[kv, s], stored.at[kv, s], in_sems.at[kv, s])

    def save(s, kv):
        return pltpu.make_async_copy(stored.at[kv, s], after_hbm.at[kv, s], out_sems.at[kv, s])

    for copy in smalls:
        copy.start()
    for kv in range(2):
        for s in range(REQS):
            load(s, kv).start()
    for copy in smalls:
        copy.wait()
    for step in range(2):
        for h in range(8):
            rows = queries[step, :, h * HD:(h + 1) * HD].astype(jnp.float32)
            query[pl.ds(step * 8 + h, REQS, stride=16), :] = rows
    for kv in range(2):
        for s in range(REQS):
            load(s, kv).wait()
            for step in range(2):
                write_row(stored, (kv, s), lengths[me * REQS + s] + step, new[step, kv, s:s + 1, :])
            save(s, kv).start()
    probs = []
    for s in range(REQS):
        scores = lax.dot_general(
            query[s * 16:(s + 1) * 16, :].astype(BF), stored[0, s], (((1,), (1,)), ((), ())),
            preferred_element_type=jnp.float32,
        ) * HD ** (-0.5)
        live = lengths[me * REQS + s] + (
            lax.broadcasted_iota(jnp.int32, scores.shape, 0) >= 8
        ).astype(jnp.int32)
        visible = lax.broadcasted_iota(jnp.int32, scores.shape, 1) <= live
        scores = jnp.where(visible, scores, -jnp.inf)
        weights = jnp.exp(scores - jnp.max(scores, axis=-1, keepdims=True))
        probs.append((weights / jnp.sum(weights, axis=-1, keepdims=True)).astype(BF))
    for s in range(REQS):
        out = jnp.dot(probs[s], stored[1, s], preferred_element_type=jnp.float32)
        att[s * 8:(s + 1) * 8, :] = out[:8]
        att[(REQS + s) * 8:(REQS + s + 1) * 8, :] = out[8:]
    for n, shift in enumerate(shifts):
        slot, _ = find_leaver(targets, me, lax.rem(me + shift, groups))
        row = att[pl.ds(pl.multiple_of((REQS + slot) * 8, 8), 8), :]
        pays[n][...] = jnp.concatenate([row] * (pays[n].shape[0] // 8), axis=0).astype(BF)
        for kv in range(2):
            if n == 0:
                whole[kv] = stored[kv, slot]
            else:
                halves[kv][...] = stored[kv, slot]
    for kv in range(2):
        for s in range(REQS):
            save(s, kv).wait()


def project_kernel(shifts, groups, parts, targets_hbm, att_ref, *rest):
    many = len(shifts)
    pays = rest[:many][::-1]
    weight_ref, out_ref, targets, att, lhs, *buffers, sem = rest[many:]
    me = lax.axis_index("inst")
    width = out_ref.shape[-1]
    if buffers:
        weight, w_sems = buffers

        def load_weight(p):
            cols = pl.ds(p * width, width)
            return pltpu.make_async_copy(weight_ref.at[:, cols], weight.at[:, cols], w_sems.at[p])

    copy = pltpu.make_async_copy(targets_hbm, targets, sem)
    copy.start()
    if buffers:
        for p in range(parts):
            load_weight(p).start()
    else:
        weight = weight_ref
    att[...] = att_ref[...]
    copy.wait()
    for n, shift in enumerate(shifts):
        _, place = find_leaver(targets, lax.rem(me + groups - shift, groups), me)
        att[pl.ds(pl.multiple_of((REQS + place) * 8, 8), 8), :] = pays[n][:16, :].astype(jnp.float32)[:8]
    for h in range(8):
        lhs[:, h * HD:(h + 1) * HD] = att[pl.ds(h, 2 * REQS, stride=8), :].astype(BF)
    for p in range(parts):
        if buffers:
            load_weight(p).wait()
        out_ref[p] = jnp.dot(
            lhs[...], weight[:, p * width:(p + 1) * width], preferred_element_type=jnp.float32
        ).astype(BF)


def sum_kernel(shares_ref, one_ref, two_ref):
    total = jnp.sum(shares_ref[...].astype(jnp.float32), axis=0)
    one_ref[...] = total[:REQS].astype(BF)
    two_ref[...] = total[REQS:].astype(BF)


def place_kernel(shifts, groups, targets_hbm, *rest):
    moved = rest[:len(shifts)]
    _, after_hbm, targets, sem, sems = rest[len(shifts):]
    me = lax.axis_index("inst")
    copy = pltpu.make_async_copy(targets_hbm, targets, sem)
    copy.start()
    copy.wait()
    copies = []
    for n, (shift, part) in enumerate(shifts):
        _, place = find_leaver(targets, lax.rem(me + groups - shift, groups), me)
        target = after_hbm.at[:, place] if part is None else after_hbm.at[part, place]
        copies.append(pltpu.make_async_copy(moved[n], target, sems.at[n]))
        copies[-1].start()
    for copy in copies:
        copy.wait()


VM = pl.BlockSpec(memory_space=pltpu.VMEM)
BF = jnp.bfloat16


def shape(dims, kind=BF):
    return jax.ShapeDtypeStruct(dims, kind)
HBM = pl.BlockSpec(memory_space=pltpu.HBM)


def limit(mib):
    return pltpu.CompilerParams(vmem_limit_bytes=mib << 20)


def on_device(caches, queries, new_entries, lengths, targets, output_weight):
    groups = lax.axis_size("inst")
    parts = lax.axis_size("tp")
    shifts = (groups // 2, 1)
    many = len(shifts)
    width = output_weight.shape[1] // parts
    perms = [[(i, (i + s) % groups) for i in range(groups)] for s in shifts]
    moves = lambda arrays: [lax.ppermute(x, "inst", perm) for x, perm in zip(arrays, perms)]

    caches, queries, new_entries, lengths, targets = [
        pltpu.with_memory_space_constraint(x, pltpu.HBM)
        for x in (caches, queries, new_entries, lengths, targets)
    ]
    *packs, att, after = pl.pallas_call(
        functools.partial(attend_kernel, shifts, groups),
        out_shape=[shape((2, CAP, HD))] + [shape((CAP, HD))] * 2 + [shape((rows, HD)) for rows in PAY_ROWS]
        + [shape((16 * REQS, HD), jnp.float32), shape(caches.shape)],
        in_specs=[HBM] * 5,
        out_specs=[VM] * (4 + many) + [HBM],
        scratch_shapes=[
            pltpu.SMEM(targets.shape, jnp.int32),
            pltpu.SMEM(lengths.shape, jnp.int32),
            pltpu.VMEM(queries.shape, BF),
            pltpu.VMEM(new_entries.shape, BF),
            pltpu.VMEM(caches.shape, BF),
            pltpu.VMEM((16 * REQS, HD), jnp.float32),
            pltpu.SemaphoreType.DMA((4,)),
            pltpu.SemaphoreType.DMA((2, REQS)),
            pltpu.SemaphoreType.DMA((2, REQS)),
        ],
        compiler_params=limit(6),
        cost_estimate=pl.CostEstimate(flops=10000000000, bytes_accessed=10**6, transcendentals=0),
        name="attend",
    )(targets, lengths, queries, new_entries, caches)
    pays = moves(packs[3:])
    whole, keys, values = [lax.ppermute(x, "inst", perms[n]) for x, n in zip(packs[:3], (0, 1, 1))]

    partial = pl.pallas_call(
        functools.partial(project_kernel, shifts, groups, parts),
        out_shape=shape((parts, 2 * REQS, width)),
        in_specs=[HBM] + [VM] * (1 + many) + [VM],
        out_specs=VM,
        scratch_shapes=[
            pltpu.SMEM(targets.shape, jnp.int32),
            pltpu.VMEM((16 * REQS, HD), jnp.float32),
            pltpu.VMEM((2 * REQS, 8 * HD), BF),
            pltpu.SemaphoreType.DMA,
        ],
        compiler_params=limit(20),
        cost_estimate=pl.CostEstimate(flops=1000000000, bytes_accessed=10**6, transcendentals=0),
        name="project",
    )(targets, att, *pays[::-1], output_weight)
    shares = lax.all_to_all(partial, "tp", 0, 0)

    one, two = pl.pallas_call(
        sum_kernel,
        out_shape=[shape((REQS, width))] * 2,
        in_specs=[VM],
        out_specs=[VM] * 2,
        compiler_params=limit(4),
        name="sum",
    )(shares)

    def place(plan, moved, after, hint):
        return pl.pallas_call(
            functools.partial(place_kernel, plan, groups),
            out_shape=shape(caches.shape),
            in_specs=[HBM] + [VM] * len(plan) + [HBM],
            out_specs=HBM,
            input_output_aliases={1 + len(plan): 0},
            scratch_shapes=[
                pltpu.SMEM(targets.shape, jnp.int32),
                pltpu.SemaphoreType.DMA,
                pltpu.SemaphoreType.DMA((len(plan),)),
            ],
            compiler_params=limit(4),
            cost_estimate=hint,
            name="place",
        )(targets, *moved, after)

    hint = pl.CostEstimate(flops=2000000000, bytes_accessed=10**6, transcendentals=0)
    after = place([(1, 0)], [keys], after, hint)
    after = place([(1, 1), (groups // 2, None)], [values, whole], after, None)
    return one, two, after


def solution(mesh):
    placed = (
        P(None, "inst", None, "tp"),
        P(None, "inst", "tp"),
        P(None, None, "inst", "tp"),
        P(),
        P(),
        P("tp", None),
    )
    return jax.shard_map(
        on_device,
        mesh=mesh,
        in_specs=placed,
        out_specs=(P("inst", "tp"), P("inst", "tp"), P(None, "inst", None, "tp")),
        check_vma=False,
    )
```

time: 70.8 us -> 34.8 us (0.49)
  the two profiles are of different devices: /device:TPU:1 before, /device:TPU:2 now
where the time goes in v3:
time: 34.8 us; the launch traced here: 34.5 us
  starting transfers between devices  16.5 us (47%)
  Pallas kernels  8.79 us (25%)
  waiting for transfers between devices  8.5 us (24%)
  between operations  0.67 us (2%)
    ppermute x2, starting transfers between devices, on_device(): lax.ppermute(x, 'inst', perm)  8.84 us
    ppermute x3, waiting for transfers between devices, on_device(): lax.ppermute(x, 'inst', perms[n])  5.32 us
    all_to_all x1, starting transfers between devices, on_device(): shares = lax.all_to_all(partial, 'tp', 0, 0)  4.84 us
    pallas_call x1, Pallas kernels, on_device(): pl.pallas_call(functools.partial(project_kernel, shifts, groups, parts),...  2.9 us
    all_to_all x1, waiting for transfers between devices, on_device(): shares = lax.all_to_all(partial, 'tp', 0, 0)  2.88 us
    ppermute x3, starting transfers between devices, on_device(): lax.ppermute(x, 'inst', perms[n])  2.86 us
    pallas_call x2, Pallas kernels, place(): pl.pallas_call(functools.partial(place_kernel, plan, groups), out_shape=s...  2.83 us
    pallas_call x1, Pallas kernels, on_device(): pl.pallas_call(functools.partial(attend_kernel, shifts, groups), out_shap...  2.45 us
  transfers between devices with their start and end apart: 6, of which 3 were waited for; matrix products, arithmetic and copies ran while one was open for 0% of the time, Pallas kernels for 14%

profile of v3, /device:TPU:2, one launch (start us, length us, event | category | flops | bytes accessed | tf_op | source)
XLA Modules:
  0.0 34.5 jit_solution(17176293306788420175)
XLA Ops:
  0.6 0.0 copy-start
  0.6 2.4 %attend.1 = (bf16[2,512,128]{2,1,0:T(8,128)(2,1)S(1)}, bf16[512,128]{1,0:T(8,128)(2,1)S(1)}, bf16[512,128]{1,0:T(8,128)(2,1)S(1)}, bf16[16,128]{1,0:T(8,128)(2,1...) custom-call(s32[128]{0:T(128)} %targets_hbm.7, s32[128]{0:T(128)} %lengths_hbm.1, ...), custom_call_target="tpu_custom_call" | custom-call | flops 10000000000 | bytes 1000000 | tf_op jit(solution)/shard_map/attend/pallas_call | solution.py:195
  3.1 1.7 %collective-permute-start = (bf16[256,128]{1,0:T(8,128)(2,1)S(1)}, bf16[256,128]{1,0:T(8,128)(2,1)S(1)}, u32[]{:S(2)}, u32[]{:S(2)}) collective-permute-start(bf16[256,128]{1,0:T(8,128)(2,1)S(1)} %get-tuple-element.13), channel_id=1, source_target_pairs={{0,8},{8,16},{16,24},{24,32},{32,40},{40,48},{48,56},{56,64},{64,7... | collective-permute-start | bytes 196616 | tf_op jit(solution)/shard_map/ppermute | solution.py:189
  4.8 1.6 %collective-permute-start.4 = (bf16[512,128]{1,0:T(8,128)(2,1)S(1)}, bf16[512,128]{1,0:T(8,128)(2,1)S(1)}, u32[]{:S(2)}, u32[]{:S(2)}) collective-permute-start(bf16[512,128]{1,0:T(8,128)(2,1)S(1)} %get-tuple-element.19), channel_id=1, source_target_pairs={{0,8},{8,16},{16,24},{24,32},{32,40},{40,48},{48,56},{56,64},{64,7... | collective-permute-start | bytes 393224 | tf_op jit(solution)/shard_map/ppermute | solution.py:217
  6.3 7.2 %collective-permute-start.1 = (bf16[16,128]{1,0:T(8,128)(2,1)S(1)}, bf16[16,128]{1,0:T(8,128)(2,1)S(1)}, u32[]{:S(2)}, u32[]{:S(2)}) collective-permute-start(bf16[16,128]{1,0:T(8,128)(2,1)S(1)} %get-tuple-element.14), channel_id=1, source_target_pairs={{0,128},{8,136},{16,144},{24,152},{32,160},{40,168},{48,176},{56,1... | collective-permute-start | bytes 12296 | tf_op jit(solution)/shard_map/ppermute | solution.py:189
  13.5 1.3 %collective-permute-start.2 = (bf16[512,128]{1,0:T(8,128)(2,1)S(1)}, bf16[512,128]{1,0:T(8,128)(2,1)S(1)}, u32[]{:S(2)}, u32[]{:S(2)}) collective-permute-start(bf16[512,128]{1,0:T(8,128)(2,1)S(1)} %get-tuple-element.17), channel_id=1, source_target_pairs={{0,8},{8,16},{16,24},{24,32},{32,40},{40,48},{48,56},{56,64},{64,7... | collective-permute-start | bytes 393224 | tf_op jit(solution)/shard_map/ppermute | solution.py:217
  14.8 0.0 collective-permute-start.3
  14.8 0.3 collective-permute-done.1.rest_1_
  15.1 0.0 collective-permute-done.rest_0_
  15.1 0.0 copy-done
  15.1 2.9 %project.1 = bf16[8,8,640]{2,1,0:T(8,128)(2,1)} custom-call(s32[128]{0:T(128)} %targets_hbm.7, f32[64,128]{1,0:T(8,128)S(1)} %get-tuple-element.12.att_ref, bf16[256,128]{1,0:T(8,128)(2,1)S(1)} %collective-permute-done.rest_0_, bf16[16,128]{1,0:T(8,128)(2,1)S(1)} %collective-permute-done.1.rest_1_, bf16[1024,5120]{1,0:T(8,128)(2,1)S(1)} %copy-done), custom_call_target="tpu_custom_call" | custom-call | flops 1000000000 | bytes 1000000 | tf_op jit(solution)/shard_map/project/pallas_call | solution.py:219
  18.0 4.8 %all-to-all-start = ((bf16[8,8,640]{2,1,0:T(8,128)(2,1)}), bf16[8,8,640]{2,1,0:T(8,128)(2,1)S(1)}, u32[]{:S(2)}, u32[]{:S(2)}) async-start(bf16[8,8,640]{2,1,0:T(8,128)(2,1)} %project.1), calls=%async_computation | async-start | bytes 163840 | tf_op jit(solution)/shard_map/all_to_all | solution.py:234
  22.9 0.0 collective-permute-done.4.rest_0_
  22.9 1.4 %place.2.rest_2_ = bf16[2,4,512,128]{3,2,1,0:T(8,128)(2,1)} custom-call(s32[128]{0:T(128)} %targets_hbm.7, bf16[512,128]{1,0:T(8,128)(2,1)S(1)} %collective-permute-done.4.rest_0_, bf16[2,4,512,128]{3,2,1,0:T(8,128)(2,1)} %get-tuple-element.20.rest_1_), custom_call_target="tpu_custom_call", output_to_operand_aliasing={{}: (2, {})} | custom-call | flops 2000000000 | bytes 1000000 | tf_op jit(solution)/shard_map/place/pallas_call | solution.py:246
  24.2 2.9 %all-to-all-done.shares_ref = bf16[8,8,640]{2,1,0:T(8,128)(2,1)S(1)} async-done(((bf16[8,8,640]{2,1,0:T(8,128)(2,1)}), bf16[8,8,640]{2,1,0:T(8,128)(2,1)S(1)}, u32[]{:S(2)}, u32[]{:S(2)}) %all-to-all-start) | async-done | bytes 81952 | tf_op jit(solution)/shard_map/all_to_all | solution.py:234
  27.1 0.6 %sum.1 = (bf16[4,640]{1,0:T(4,128)(2,1)}, bf16[4,640]{1,0:T(4,128)(2,1)}) custom-call(bf16[8,8,640]{2,1,0:T(8,128)(2,1)S(1)} %all-to-all-done.shares_ref), custom_call_target="tpu_custom_call" | custom-call | tf_op jit(solution)/shard_map/sum/pallas_call | solution.py:236
  27.7 5.3 %collective-permute-done.2.rest_0_ = bf16[512,128]{1,0:T(8,128)(2,1)S(1)} collective-permute-done((bf16[512,128]{1,0:T(8,128)(2,1)S(1)}, bf16[512,128]{1,0:T(8,128)(2,1)S(1)}, u32[]{:S(2)}, u32[]{:S(2)}) %collective-permute-start.2) | collective-permute-done | bytes 131104 | tf_op jit(solution)/shard_map/ppermute | solution.py:217
  33.0 0.0 collective-permute-done.3.rest_1_
  33.0 1.5 %place.3 = bf16[2,4,512,128]{3,2,1,0:T(8,128)(2,1)} custom-call(s32[128]{0:T(128)} %targets_hbm.7, bf16[512,128]{1,0:T(8,128)(2,1)S(1)} %collective-permute-done.2.rest_0_, bf16[2,512,128]{2,1,0:T(8,128)(2,1)S(1)} %collective-permute-done.3.rest_1_, bf16[2,4,512,128]{3,2,1,0:T(8,128)(2,1)} %place.2.rest_2_), custom_call_target="tpu_custom_call", output_to_operand_aliasing={{}: (3, {})} | custom-call | tf_op jit(solution)/shard_map/place/pallas_call | solution.py:246
Async XLA Ops:
  0.6 14.5 %copy-start = (bf16[1024,5120]{1,0:T(8,128)(2,1)S(1)}, bf16[1024,5120]{1,0:T(8,128)(2,1)}, u32[]{:S(2)}) copy-start(bf16[1024,5120]{1,0:T(8,128)(2,1)} %rest_2_.1) | copy-start | bytes 31457284
  3.1 12.0 %collective-permute-start = (bf16[256,128]{1,0:T(8,128)(2,1)S(1)}, bf16[256,128]{1,0:T(8,128)(2,1)S(1)}, u32[]{:S(2)}, u32[]{:S(2)}) collective-permute-start(bf16[256,128]{1,0:T(8,128)(2,1)S(1)} %get-tuple-element.13), channel_id=1, source_target_pairs={{0,8},{8,16},{16,24},{24,32},{32,40},{40,48},{48,56},{56,64},{64,7... | collective-permute-start | bytes 196616 | tf_op jit(solution)/shard_map/ppermute | solution.py:189
  4.8 18.1 %collective-permute-start.4 = (bf16[512,128]{1,0:T(8,128)(2,1)S(1)}, bf16[512,128]{1,0:T(8,128)(2,1)S(1)}, u32[]{:S(2)}, u32[]{:S(2)}) collective-permute-start(bf16[512,128]{1,0:T(8,128)(2,1)S(1)} %get-tuple-element.19), channel_id=1, source_target_pairs={{0,8},{8,16},{16,24},{24,32},{32,40},{40,48},{48,56},{56,64},{64,7... | collective-permute-start | bytes 393224 | tf_op jit(solution)/shard_map/ppermute | solution.py:217
  6.3 8.8 %collective-permute-start.1 = (bf16[16,128]{1,0:T(8,128)(2,1)S(1)}, bf16[16,128]{1,0:T(8,128)(2,1)S(1)}, u32[]{:S(2)}, u32[]{:S(2)}) collective-permute-start(bf16[16,128]{1,0:T(8,128)(2,1)S(1)} %get-tuple-element.14), channel_id=1, source_target_pairs={{0,128},{8,136},{16,144},{24,152},{32,160},{40,168},{48,176},{56,1... | collective-permute-start | bytes 12296 | tf_op jit(solution)/shard_map/ppermute | solution.py:189
  13.5 19.5 %collective-permute-start.2 = (bf16[512,128]{1,0:T(8,128)(2,1)S(1)}, bf16[512,128]{1,0:T(8,128)(2,1)S(1)}, u32[]{:S(2)}, u32[]{:S(2)}) collective-permute-start(bf16[512,128]{1,0:T(8,128)(2,1)S(1)} %get-tuple-element.17), channel_id=1, source_target_pairs={{0,8},{8,16},{16,24},{24,32},{32,40},{40,48},{48,56},{56,64},{64,7... | collective-permute-start | bytes 393224 | tf_op jit(solution)/shard_map/ppermute | solution.py:217
  14.8 18.2 %collective-permute-start.3 = (bf16[2,512,128]{2,1,0:T(8,128)(2,1)S(1)}, bf16[2,512,128]{2,1,0:T(8,128)(2,1)S(1)}, u32[]{:S(2)}, u32[]{:S(2)}) collective-permute-start(bf16[2,512,128]{2,1,0:T(8,128)(2,1)S(1)} %get-tuple-element.18), channel_id=1, source_target_pairs={{0,128},{8,136},{16,144},{24,152},{32,160},{40,168},{48,176},{56,1... | collective-permute-start | bytes 786440 | tf_op jit(solution)/shard_map/ppermute | solution.py:217
  18.0 9.1 %all-to-all-start = ((bf16[8,8,640]{2,1,0:T(8,128)(2,1)}), bf16[8,8,640]{2,1,0:T(8,128)(2,1)S(1)}, u32[]{:S(2)}, u32[]{:S(2)}) async-start(bf16[8,8,640]{2,1,0:T(8,128)(2,1)} %project.1), calls=%async_computation | async-start | bytes 163840 | tf_op jit(solution)/shard_map/all_to_all | solution.py:234

commit v4 on v3

v4 whole, which is shorter than its diff:
```python
import functools

import jax
import jax.numpy as jnp
from jax import lax
from jax.experimental import pallas as pl
from jax.experimental.pallas import tpu as pltpu
from jax.sharding import PartitionSpec as P

HD = 128
REQS = 4
CAP = 512
TILE = 16
FAR = 64
NEAR = 128


def bcast_rows(row, rows):
    return jnp.broadcast_to(row, (rows, row.shape[-1]))


def write_row(ref, lead, position, row):
    base = pl.multiple_of((position // TILE) * TILE, TILE)
    window = ref[lead + (pl.ds(base, TILE), slice(None))]
    at = lax.broadcasted_iota(jnp.int32, window.shape, 0) == position - base
    ref[lead + (pl.ds(base, TILE), slice(None))] = jnp.where(at, bcast_rows(row, TILE), window)


def find_leaver(targets_ref, source_inst, target_inst):
    slot = jnp.int32(0)
    place = jnp.int32(0)
    for j in range(REQS):
        t = targets_ref[source_inst * REQS + j]
        hit = t // REQS == target_inst
        slot = jnp.where(hit, j, slot)
        place = jnp.where(hit, t % REQS, place)
    return slot, place


def attend_kernel(shifts, groups, targets_hbm, lengths_hbm, queries_hbm, new_hbm, caches_hbm, *rest):
    lead_far, lead_near, tail_near, tail_far = rest[:4]
    (places, att, after_hbm, targets, lengths, queries, new, stored, query, small_sems, in_sems,
     out_sems) = rest[4:]
    me = lax.axis_index("inst")
    smalls = [
        pltpu.make_async_copy(source, target, small_sems.at[n])
        for n, (source, target) in enumerate(
            [(lengths_hbm, lengths), (new_hbm, new), (targets_hbm, targets), (queries_hbm, queries)]
        )
    ]

    def load(s, kv):
        return pltpu.make_async_copy(caches_hbm.at[kv, s], stored.at[kv, s], in_sems.at[kv, s])

    def save(s, kv):
        return pltpu.make_async_copy(stored.at[kv, s], after_hbm.at[kv, s], out_sems.at[kv, s])

    for copy in smalls:
        copy.start()
    for kv in range(2):
        for s in range(REQS):
            load(s, kv).start()
    for copy in smalls:
        copy.wait()
    slots = [find_leaver(targets, me, lax.rem(me + shift, groups))[0] for shift in shifts]
    for n, shift in enumerate(shifts):
        _, place = find_leaver(targets, lax.rem(me + groups - shift, groups), me)
        places[n:n + 1, :] = jnp.full((1, HD), place.astype(jnp.float32))
    for step in range(2):
        for h in range(8):
            rows = queries[step, :, h * HD:(h + 1) * HD].astype(jnp.float32)
            query[pl.ds(step * 8 + h, REQS, stride=16), :] = rows
    for kv in range(2):
        for s in range(REQS):
            load(s, kv).wait()
            for step in range(2):
                write_row(stored, (kv, s), lengths[me * REQS + s] + step, new[step, kv, s:s + 1, :])
            save(s, kv).start()
    probs = []
    for s in range(REQS):
        scores = lax.dot_general(
            query[s * 16:(s + 1) * 16, :].astype(BF), stored[0, s], (((1,), (1,)), ((), ())),
            preferred_element_type=jnp.float32,
        ) * HD ** (-0.5)
        live = lengths[me * REQS + s] + (
            lax.broadcasted_iota(jnp.int32, scores.shape, 0) >= 8
        ).astype(jnp.int32)
        visible = lax.broadcasted_iota(jnp.int32, scores.shape, 1) <= live
        scores = jnp.where(visible, scores, -jnp.inf)
        weights = jnp.exp(scores - jnp.max(scores, axis=-1, keepdims=True))
        probs.append((weights / jnp.sum(weights, axis=-1, keepdims=True)).astype(BF))
    for s in range(REQS):
        out = jnp.dot(probs[s], stored[1, s], preferred_element_type=jnp.float32)
        att[s * 8:(s + 1) * 8, :] = out[:8]
        att[(REQS + s) * 8:(REQS + s + 1) * 8, :] = out[8:]
    for shift, slot, lead in zip(shifts, slots, (lead_far, lead_near)):
        row = att[pl.ds(pl.multiple_of((REQS + slot) * 8, 8), 8), :]
        lead[:TILE, :] = jnp.concatenate([row, row], axis=0).astype(BF)
        if shift == 1:
            lead[TILE:TILE + CAP, :] = stored[0, slot]
            lead[TILE + CAP:, :] = stored[1, slot, :NEAR]
            tail_near[...] = stored[1, slot, NEAR:]
        else:
            for kv in range(2):
                lead[TILE + kv * FAR:TILE + (kv + 1) * FAR, :] = stored[kv, slot, :FAR]
                tail_far[kv * (CAP - FAR):(kv + 1) * (CAP - FAR), :] = stored[kv, slot, FAR:]
    for kv in range(2):
        for s in range(REQS):
            save(s, kv).wait()


def place_of(places_ref, n):
    return jnp.max(places_ref[n:n + 1, :]).astype(jnp.int32)


def project_kernel(parts, places_ref, att_ref, near_ref, far_ref, weight_ref, out_ref, att, lhs):
    width = out_ref.shape[-1]
    att[...] = att_ref[...]
    for n, pay in enumerate((far_ref, near_ref)):
        place = place_of(places_ref, n)
        att[pl.ds(pl.multiple_of((REQS + place) * 8, 8), 8), :] = pay[:TILE, :].astype(jnp.float32)[:8]
    for h in range(8):
        lhs[:, h * HD:(h + 1) * HD] = att[pl.ds(h, 2 * REQS, stride=8), :].astype(BF)
    for p in range(parts):
        out_ref[p] = jnp.dot(
            lhs[...], weight_ref[:, p * width:(p + 1) * width], preferred_element_type=jnp.float32
        ).astype(BF)


def start_placing(plan, places_ref, moved, after_hbm, sems):
    pairs = []
    for (n, pieces), source in zip(plan, moved):
        place = place_of(places_ref, n)
        for first, rows, kv, position in pieces:
            pairs.append((source.at[pl.ds(first, rows)], after_hbm.at[kv, place, pl.ds(position, rows)]))
    copies = [pltpu.make_async_copy(a, b, sems.at[n]) for n, (a, b) in enumerate(pairs)]
    for copy in copies:
        copy.start()
    return copies


def place_kernel(plan, places_ref, *rest):
    moved = rest[:len(plan)]
    _, after_hbm, sems = rest[len(plan):]
    for copy in start_placing(plan, places_ref, moved, after_hbm, sems):
        copy.wait()


def finish_kernel(plan, places_ref, *rest):
    moved = rest[:len(plan)]
    _, shares_ref, after_hbm, one_ref, two_ref, sems = rest[len(plan):]
    copies = start_placing(plan, places_ref, moved, after_hbm, sems)
    total = jnp.sum(shares_ref[...].astype(jnp.float32), axis=0)
    one_ref[...] = total[:REQS].astype(BF)
    two_ref[...] = total[REQS:].astype(BF)
    for copy in copies:
        copy.wait()


def pieces_of(first, rows, kv, position, cuts):
    step = rows // cuts
    return [(first + c * step, step, kv, position + c * step) for c in range(cuts)]


VM = pl.BlockSpec(memory_space=pltpu.VMEM)
HBM = pl.BlockSpec(memory_space=pltpu.HBM)
BF = jnp.bfloat16


def shape(dims, kind=BF):
    return jax.ShapeDtypeStruct(dims, kind)


def limit(mib):
    return pltpu.CompilerParams(vmem_limit_bytes=mib << 20)


def on_device(caches, queries, new_entries, lengths, targets, output_weight):
    groups = lax.axis_size("inst")
    parts = lax.axis_size("tp")
    shifts = (groups // 2, 1)
    many = len(shifts)
    width = output_weight.shape[1] // parts
    perms = [[(i, (i + s) % groups) for i in range(groups)] for s in shifts]

    caches, queries, new_entries, lengths, targets = [
        pltpu.with_memory_space_constraint(x, pltpu.HBM)
        for x in (caches, queries, new_entries, lengths, targets)
    ]
    *packs, places, att, after = pl.pallas_call(
        functools.partial(attend_kernel, shifts, groups),
        out_shape=[shape((TILE + 2 * FAR, HD)), shape((TILE + CAP + NEAR, HD)), shape((CAP - NEAR, HD)),
                   shape((2 * (CAP - FAR), HD))]
        + [shape((8, HD), jnp.float32), shape((16 * REQS, HD), jnp.float32), shape(caches.shape)],
        in_specs=[HBM] * 5,
        out_specs=[VM] * 6 + [HBM],
        scratch_shapes=[
            pltpu.SMEM(targets.shape, jnp.int32),
            pltpu.SMEM(lengths.shape, jnp.int32),
            pltpu.VMEM(queries.shape, BF),
            pltpu.VMEM(new_entries.shape, BF),
            pltpu.VMEM(caches.shape, BF),
            pltpu.VMEM((16 * REQS, HD), jnp.float32),
            pltpu.SemaphoreType.DMA((4,)),
            pltpu.SemaphoreType.DMA((2, REQS)),
            pltpu.SemaphoreType.DMA((2, REQS)),
        ],
        compiler_params=limit(6),
        cost_estimate=pl.CostEstimate(flops=10000000000, bytes_accessed=10**6, transcendentals=0),
        name="attend",
    )(targets, lengths, queries, new_entries, caches)
    lead_far, lead_near, tail_near, tail_far = [
        lax.ppermute(x, "inst", perms[n]) for x, n in zip(packs, (0, 1, 1, 0))
    ]

    partial = pl.pallas_call(
        functools.partial(project_kernel, parts),
        out_shape=shape((parts, 2 * REQS, width)),
        in_specs=[VM] * 5,
        out_specs=VM,
        scratch_shapes=[
            pltpu.VMEM((16 * REQS, HD), jnp.float32),
            pltpu.VMEM((2 * REQS, 8 * HD), BF),
        ],
        compiler_params=limit(20),
        cost_estimate=pl.CostEstimate(flops=1000000000, bytes_accessed=10**6, transcendentals=0),
        name="project",
    )(places, att, lead_near, lead_far, output_weight)
    shares = lax.all_to_all(partial, "tp", 0, 0)

    plan = [
        (1, pieces_of(TILE, CAP, 0, 0, 2) + pieces_of(TILE + CAP, NEAR, 1, 0, 1)),
        (0, [piece for kv in range(2) for piece in pieces_of(TILE + kv * FAR, FAR, kv, 0, 1)]),
    ]
    after = pl.pallas_call(
        functools.partial(place_kernel, plan),
        out_shape=shape(caches.shape),
        in_specs=[VM] * 3 + [HBM],
        out_specs=HBM,
        input_output_aliases={3: 0},
        scratch_shapes=[pltpu.SemaphoreType.DMA((sum(len(pieces) for _, pieces in plan),))],
        compiler_params=limit(4),
        cost_estimate=pl.CostEstimate(flops=2000000000, bytes_accessed=10**6, transcendentals=0),
        name="place",
    )(places, lead_near, lead_far, after)

    rest = CAP - FAR
    plan = [
        (1, pieces_of(0, CAP - NEAR, 1, NEAR, 1)),
        (0, [piece for kv in range(2) for piece in pieces_of(kv * rest, rest, kv, FAR, 2)]),
    ]
    after, one, two = pl.pallas_call(
        functools.partial(finish_kernel, plan),
        out_shape=[shape(caches.shape)] + [shape((REQS, width))] * 2,
        in_specs=[VM] * 3 + [HBM, VM],
        out_specs=[HBM, VM, VM],
        input_output_aliases={3: 0},
        scratch_shapes=[pltpu.SemaphoreType.DMA((sum(len(pieces) for _, pieces in plan),))],
        compiler_params=limit(4),
        name="finish",
    )(places, tail_near, tail_far, after, shares)
    return one, two, after


def solution(mesh):
    placed = (
        P(None, "inst", None, "tp"),
        P(None, "inst", "tp"),
        P(None, None, "inst", "tp"),
        P(),
        P(),
        P("tp", None),
    )
    return jax.shard_map(
        on_device,
        mesh=mesh,
        in_specs=placed,
        out_specs=(P("inst", "tp"), P("inst", "tp"), P(None, "inst", None, "tp")),
        check_vma=False,
    )
```

time: 34.8 us -> 31.5 us (0.905)
  the two profiles are of different devices: /device:TPU:2 before, /device:TPU:24 now
where the time goes in v4:
time: 31.5 us; the launch traced here: 31.3 us
  starting transfers between devices  13.8 us (44%)
  waiting for transfers between devices  9.79 us (31%)
  Pallas kernels  7.05 us (22%)
  between operations  0.67 us (2%)
    ppermute x4, starting transfers between devices, on_device(): lax.ppermute(x, 'inst', perms[n])  9.52 us
    ppermute x4, waiting for transfers between devices, on_device(): lax.ppermute(x, 'inst', perms[n])  7.1 us
    all_to_all x1, starting transfers between devices, on_device(): shares = lax.all_to_all(partial, 'tp', 0, 0)  4.3 us
    all_to_all x1, waiting for transfers between devices, on_device(): shares = lax.all_to_all(partial, 'tp', 0, 0)  2.69 us
    pallas_call x1, Pallas kernels, on_device(): pl.pallas_call(functools.partial(attend_kernel, shifts, groups), out_shap...  2.48 us
    pallas_call x1, Pallas kernels, on_device(): pl.pallas_call(functools.partial(project_kernel, parts), out_shape=shape(...  2.28 us
    pallas_call x1, Pallas kernels, on_device(): pl.pallas_call(functools.partial(finish_kernel, plan), out_shape=[shape(c...  1.47 us
    pallas_call x1, Pallas kernels, on_device(): pl.pallas_call(functools.partial(place_kernel, plan), out_shape=shape(cac...  0.83 us
  transfers between devices with their start and end apart: 5, of which 3 were waited for; matrix products, arithmetic and copies ran while one was open for 0% of the time, Pallas kernels for 10%

profile of v4, /device:TPU:24, one launch (start us, length us, event | category | flops | bytes accessed | tf_op | source)
XLA Modules:
  0.0 31.3 jit_solution(639705355322416221)
XLA Ops:
  0.6 0.0 copy-start
  0.6 2.5 %attend.1 = (bf16[144,128]{1,0:T(8,128)(2,1)S(1)}, bf16[656,128]{1,0:T(8,128)(2,1)S(1)}, bf16[384,128]{1,0:T(8,128)(2,1)S(1)}, bf16[896,128]{1,0:T(8,128)(2,1)S(...) custom-call(s32[128]{0:T(128)} %targets_hbm.1, s32[128]{0:T(128)} %lengths_hbm.1, ...), custom_call_target="tpu_custom_call" | custom-call | flops 10000000000 | bytes 1000000 | tf_op jit(solution)/shard_map/attend/pallas_call | solution.py:190
  3.1 1.7 %collective-permute-start.2 = (bf16[656,128]{1,0:T(8,128)(2,1)S(1)}, bf16[656,128]{1,0:T(8,128)(2,1)S(1)}, u32[]{:S(2)}, u32[]{:S(2)}) collective-permute-start(bf16[656,128]{1,0:T(8,128)(2,1)S(1)} %get-tuple-element.16), channel_id=1, source_target_pairs={{0,8},{8,16},{16,24},{24,32},{32,40},{40,48},{48,56},{56,64},{64,7... | collective-permute-start | bytes 503816 | tf_op jit(solution)/shard_map/ppermute | solution.py:213
  4.8 6.3 %collective-permute-start.3 = (bf16[144,128]{1,0:T(8,128)(2,1)S(1)}, bf16[144,128]{1,0:T(8,128)(2,1)S(1)}, u32[]{:S(2)}, u32[]{:S(2)}) collective-permute-start(bf16[144,128]{1,0:T(8,128)(2,1)S(1)} %get-tuple-element.17), channel_id=1, source_target_pairs={{0,128},{8,136},{16,144},{24,152},{32,160},{40,168},{48,176},{56,1... | collective-permute-start | bytes 110600 | tf_op jit(solution)/shard_map/ppermute | solution.py:213
  11.1 1.6 %collective-permute-start = (bf16[384,128]{1,0:T(8,128)(2,1)S(1)}, bf16[384,128]{1,0:T(8,128)(2,1)S(1)}, u32[]{:S(2)}, u32[]{:S(2)}) collective-permute-start(bf16[384,128]{1,0:T(8,128)(2,1)S(1)} %get-tuple-element.14), channel_id=1, source_target_pairs={{0,8},{8,16},{16,24},{24,32},{32,40},{40,48},{48,56},{56,64},{64,7... | collective-permute-start | bytes 294920 | tf_op jit(solution)/shard_map/ppermute | solution.py:213
  12.7 0.0 collective-permute-start.1
  12.7 4.9 %collective-permute-done.3.rest_1_.far_ref = bf16[144,128]{1,0:T(8,128)(2,1)S(1)} collective-permute-done((bf16[144,128]{1,0:T(8,128)(2,1)S(1)}, bf16[144,128]{1,0:T(8,128)(2,1)S(1)}, u32[]{:S(2)}, u32[]{:S(2)}) %collective-permute-start.3) | collective-permute-done | bytes 36896 | tf_op jit(solution)/shard_map/ppermute | solution.py:213
  17.6 0.0 collective-permute-done.2.rest_0_.near_ref
  17.6 0.0 copy-done
  17.6 2.3 %project.1 = bf16[8,8,640]{2,1,0:T(8,128)(2,1)} custom-call(f32[8,128]{1,0:T(8,128)S(1)} %get-tuple-element.13.places_ref, f32[64,128]{1,0:T(8,128)S(1)} %get-tuple-element.19.att_ref, bf16[656,128]{1,0:T(8,128)(2,1)S(1)} %collective-permute-done.2.rest_0_.near_ref, bf16[144,128]{1,0:T(8,128)(2,1)S(1)} %collective-permute-done.3.rest_1_.far_ref, ...), custom_call_target="tpu_custom_call" | custom-call | flops 1000000000 | bytes 1000000 | tf_op jit(solution)/shard_map/project/pallas_call | solution.py:216
  19.9 4.3 %all-to-all-start = ((bf16[8,8,640]{2,1,0:T(8,128)(2,1)}), bf16[8,8,640]{2,1,0:T(8,128)(2,1)S(1)}, u32[]{:S(2)}, u32[]{:S(2)}) async-start(bf16[8,8,640]{2,1,0:T(8,128)(2,1)} %project.1), calls=%async_computation | async-start | bytes 163840 | tf_op jit(solution)/shard_map/all_to_all | solution.py:229
  24.2 0.8 %place.1.rest_2_ = bf16[2,4,512,128]{3,2,1,0:T(8,128)(2,1)} custom-call(f32[8,128]{1,0:T(8,128)S(1)} %get-tuple-element.13.places_ref, bf16[656,128]{1,0:T(8,128)(2,1)S(1)} %collective-permute-done.2.rest_0_.near_ref, bf16[144,128]{1,0:T(8,128)(2,1)S(1)} %collective-permute-done.3.rest_1_.far_ref, ...), custom_call_target="tpu_custom_call", output_to_operand_aliasing={{}: (3, {})} | custom-call | flops 2000000000 | bytes 1000000 | tf_op jit(solution)/shard_map/place/pallas_call | solution.py:235
  25.0 0.0 collective-permute-done.rest_0_
  25.0 2.2 %collective-permute-done.1.rest_1_ = bf16[896,128]{1,0:T(8,128)(2,1)S(1)} collective-permute-done((bf16[896,128]{1,0:T(8,128)(2,1)S(1)}, bf16[896,128]{1,0:T(8,128)(2,1)S(1)}, u32[]{:S(2)}, u32[]{:S(2)}) %collective-permute-start.1) | collective-permute-done | bytes 229408 | tf_op jit(solution)/shard_map/ppermute | solution.py:213
  27.2 2.7 %all-to-all-done.rest_3_ = bf16[8,8,640]{2,1,0:T(8,128)(2,1)S(1)} async-done(((bf16[8,8,640]{2,1,0:T(8,128)(2,1)}), bf16[8,8,640]{2,1,0:T(8,128)(2,1)S(1)}, u32[]{:S(2)}, u32[]{:S(2)}) %all-to-all-start) | async-done | bytes 81952 | tf_op jit(solution)/shard_map/all_to_all | solution.py:229
  29.9 1.5 %finish.1 = (bf16[2,4,512,128]{3,2,1,0:T(8,128)(2,1)}, bf16[4,640]{1,0:T(4,128)(2,1)}, bf16[4,640]{1,0:T(4,128)(2,1)}) custom-call(f32[8,128]{1,0:T(8,128)S(1)} %get-tuple-element.13.places_ref, bf16[384,128]{1,0:T(8,128)(2,1)S(1)} %collective-permute-done.rest_0_, ...), custom_call_target="tpu_custom_call", output_to_operand_aliasing={{0}: (3, {})} | custom-call | tf_op jit(solution)/shard_map/finish/pallas_call | solution.py:252
Async XLA Ops:
  0.6 16.9 %copy-start = (bf16[1024,5120]{1,0:T(8,128)(2,1)S(1)}, bf16[1024,5120]{1,0:T(8,128)(2,1)}, u32[]{:S(2)}) copy-start(bf16[1024,5120]{1,0:T(8,128)(2,1)} %weight_ref.1) | copy-start | bytes 31457284
  3.1 14.4 %collective-permute-start.2 = (bf16[656,128]{1,0:T(8,128)(2,1)S(1)}, bf16[656,128]{1,0:T(8,128)(2,1)S(1)}, u32[]{:S(2)}, u32[]{:S(2)}) collective-permute-start(bf16[656,128]{1,0:T(8,128)(2,1)S(1)} %get-tuple-element.16), channel_id=1, source_target_pairs={{0,8},{8,16},{16,24},{24,32},{32,40},{40,48},{48,56},{56,64},{64,7... | collective-permute-start | bytes 503816 | tf_op jit(solution)/shard_map/ppermute | solution.py:213
  4.8 12.8 %collective-permute-start.3 = (bf16[144,128]{1,0:T(8,128)(2,1)S(1)}, bf16[144,128]{1,0:T(8,128)(2,1)S(1)}, u32[]{:S(2)}, u32[]{:S(2)}) collective-permute-start(bf16[144,128]{1,0:T(8,128)(2,1)S(1)} %get-tuple-element.17), channel_id=1, source_target_pairs={{0,128},{8,136},{16,144},{24,152},{32,160},{40,168},{48,176},{56,1... | collective-permute-start | bytes 110600 | tf_op jit(solution)/shard_map/ppermute | solution.py:213
  11.1 13.9 %collective-permute-start = (bf16[384,128]{1,0:T(8,128)(2,1)S(1)}, bf16[384,128]{1,0:T(8,128)(2,1)S(1)}, u32[]{:S(2)}, u32[]{:S(2)}) collective-permute-start(bf16[384,128]{1,0:T(8,128)(2,1)S(1)} %get-tuple-element.14), channel_id=1, source_target_pairs={{0,8},{8,16},{16,24},{24,32},{32,40},{40,48},{48,56},{56,64},{64,7... | collective-permute-start | bytes 294920 | tf_op jit(solution)/shard_map/ppermute | solution.py:213
  12.7 14.5 %collective-permute-start.1 = (bf16[896,128]{1,0:T(8,128)(2,1)S(1)}, bf16[896,128]{1,0:T(8,128)(2,1)S(1)}, u32[]{:S(2)}, u32[]{:S(2)}) collective-permute-start(bf16[896,128]{1,0:T(8,128)(2,1)S(1)} %get-tuple-element.15), channel_id=1, source_target_pairs={{0,128},{8,136},{16,144},{24,152},{32,160},{40,168},{48,176},{56,1... | collective-permute-start | bytes 688136 | tf_op jit(solution)/shard_map/ppermute | solution.py:213
  19.9 10.0 %all-to-all-start = ((bf16[8,8,640]{2,1,0:T(8,128)(2,1)}), bf16[8,8,640]{2,1,0:T(8,128)(2,1)S(1)}, u32[]{:S(2)}, u32[]{:S(2)}) async-start(bf16[8,8,640]{2,1,0:T(8,128)(2,1)} %project.1), calls=%async_computation | async-start | bytes 163840 | tf_op jit(solution)/shard_map/all_to_all | solution.py:229

commit v5 on v4

--- a/solution.py
+++ b/solution.py
@@ -19,11 +19,18 @@
     return jnp.broadcast_to(row, (rows, row.shape[-1]))
 
 
-def write_row(ref, lead, position, row):
-    base = pl.multiple_of((position // TILE) * TILE, TILE)
-    window = ref[lead + (pl.ds(base, TILE), slice(None))]
-    at = lax.broadcasted_iota(jnp.int32, window.shape, 0) == position - base
-    ref[lead + (pl.ds(base, TILE), slice(None))] = jnp.where(at, bcast_rows(row, TILE), window)
+def write_tokens(ref, kv, lengths, new):
+    writes = []
+    for s, length in enumerate(lengths):
+        for position in (length, length + 1):
+            base = pl.multiple_of((position // TILE) * TILE, TILE)
+            window = ref[kv, s, pl.ds(base, TILE), :]
+            row = lax.broadcasted_iota(jnp.int32, window.shape, 0) + base
+            for step in range(2):
+                window = jnp.where(row == length + step, bcast_rows(new[step, kv, s:s + 1, :], TILE), window)
+            writes.append((s, base, window))
+    for s, base, window in writes:
+        ref[kv, s, pl.ds(base, TILE), :] = window
 
 
 def find_leaver(targets_ref, source_inst, target_inst):
@@ -39,8 +46,7 @@
 
 def attend_kernel(shifts, groups, targets_hbm, lengths_hbm, queries_hbm, new_hbm, caches_hbm, *rest):
     lead_far, lead_near, tail_near, tail_far = rest[:4]
-    (places, att, after_hbm, targets, lengths, queries, new, stored, query, small_sems, in_sems,
-     out_sems) = rest[4:]
+    places, att, stored, targets, lengths, queries, new, query, small_sems, in_sems = rest[4:]
     me = lax.axis_index("inst")
     smalls = [
         pltpu.make_async_copy(source, target, small_sems.at[n])
@@ -51,9 +57,6 @@
 
     def load(s, kv):
         return pltpu.make_async_copy(caches_hbm.at[kv, s], stored.at[kv, s], in_sems.at[kv, s])
-
-    def save(s, kv):
-        return pltpu.make_async_copy(stored.at[kv, s], after_hbm.at[kv, s], out_sems.at[kv, s])
 
     for copy in smalls:
         copy.start()
@@ -70,19 +73,18 @@
         for h in range(8):
             rows = queries[step, :, h * HD:(h + 1) * HD].astype(jnp.float32)
             query[pl.ds(step * 8 + h, REQS, stride=16), :] = rows
+    own_lengths = [lengths[me * REQS + s] for s in range(REQS)]
     for kv in range(2):
         for s in range(REQS):
             load(s, kv).wait()
-            for step in range(2):
-                write_row(stored, (kv, s), lengths[me * REQS + s] + step, new[step, kv, s:s + 1, :])
-            save(s, kv).start()
+        write_tokens(stored, kv, own_lengths, new)
     probs = []
     for s in range(REQS):
         scores = lax.dot_general(
             query[s * 16:(s + 1) * 16, :].astype(BF), stored[0, s], (((1,), (1,)), ((), ())),
             preferred_element_type=jnp.float32,
         ) * HD ** (-0.5)
-        live = lengths[me * REQS + s] + (
+        live = own_lengths[s] + (
             lax.broadcasted_iota(jnp.int32, scores.shape, 0) >= 8
         ).astype(jnp.int32)
         visible = lax.broadcasted_iota(jnp.int32, scores.shape, 1) <= live
@@ -104,27 +106,28 @@
             for kv in range(2):
                 lead[TILE + kv * FAR:TILE + (kv + 1) * FAR, :] = stored[kv, slot, :FAR]
                 tail_far[kv * (CAP - FAR):(kv + 1) * (CAP - FAR), :] = stored[kv, slot, FAR:]
-    for kv in range(2):
-        for s in range(REQS):
-            save(s, kv).wait()
 
 
 def place_of(places_ref, n):
     return jnp.max(places_ref[n:n + 1, :]).astype(jnp.int32)
 
 
-def project_kernel(parts, places_ref, att_ref, near_ref, far_ref, weight_ref, out_ref, att, lhs):
+def project_kernel(parts, places_ref, att_ref, near_ref, far_ref, weight_ref, out_ref, lhs):
     width = out_ref.shape[-1]
-    att[...] = att_ref[...]
-    for n, pay in enumerate((far_ref, near_ref)):
-        place = place_of(places_ref, n)
-        att[pl.ds(pl.multiple_of((REQS + place) * 8, 8), 8), :] = pay[:TILE, :].astype(jnp.float32)[:8]
+    rows = lax.broadcasted_iota(jnp.int32, (2 * REQS, HD), 0).astype(jnp.float32)
+    pays = [pay[:TILE, :].astype(jnp.float32) for pay in (far_ref, near_ref)]
     for h in range(8):
-        lhs[:, h * HD:(h + 1) * HD] = att[pl.ds(h, 2 * REQS, stride=8), :].astype(BF)
-    for p in range(parts):
-        out_ref[p] = jnp.dot(
-            lhs[...], weight_ref[:, p * width:(p + 1) * width], preferred_element_type=jnp.float32
+        head = att_ref[pl.ds(h, 2 * REQS, stride=8), :]
+        for n, pay in enumerate(pays):
+            at = rows == bcast_rows(places_ref[n:n + 1, :] + REQS, 2 * REQS)
+            head = jnp.where(at, bcast_rows(pay[h:h + 1], 2 * REQS), head)
+        lhs[:, h * HD:(h + 1) * HD] = head.astype(BF)
+    for p in range(0, parts, 2):
+        both = jnp.dot(
+            lhs[...], weight_ref[:, p * width:(p + 2) * width], preferred_element_type=jnp.float32
         ).astype(BF)
+        out_ref[p] = both[:, :width]
+        out_ref[p + 1] = both[:, width:]
 
 
 def start_placing(plan, places_ref, moved, after_hbm, sems):
@@ -139,20 +142,33 @@
     return copies
 
 
-def place_kernel(plan, places_ref, *rest):
-    moved = rest[:len(plan)]
-    _, after_hbm, sems = rest[len(plan):]
-    for copy in start_placing(plan, places_ref, moved, after_hbm, sems):
+def place_kernel(plan, places_ref, near_ref, far_ref, stored, after_hbm, sems, stay_sems):
+    copies = start_placing(plan, places_ref, (near_ref, far_ref), after_hbm, sems)
+    taken = [place_of(places_ref, n) for n in range(2)]
+
+    def for_staying(act):
+        for s in range(REQS):
+            @pl.when((taken[0] != s) & (taken[1] != s))
+            def _():
+                for kv in range(2):
+                    act(pltpu.make_async_copy(stored.at[kv, s], after_hbm.at[kv, s], stay_sems.at[kv, s]))
+
+    for_staying(lambda copy: copy.start())
+    for copy in copies:
         copy.wait()
+    for_staying(lambda copy: copy.wait())
 
 
 def finish_kernel(plan, places_ref, *rest):
     moved = rest[:len(plan)]
-    _, shares_ref, after_hbm, one_ref, two_ref, sems = rest[len(plan):]
+    _, shares_ref, after_hbm, one_hbm, two_hbm, one, two, sems, out_sems = rest[len(plan):]
     copies = start_placing(plan, places_ref, moved, after_hbm, sems)
     total = jnp.sum(shares_ref[...].astype(jnp.float32), axis=0)
-    one_ref[...] = total[:REQS].astype(BF)
-    two_ref[...] = total[REQS:].astype(BF)
+    one[...] = total[:REQS].astype(BF)
+    two[...] = total[REQS:].astype(BF)
+    for n, (source, target) in enumerate(((one, one_hbm), (two, two_hbm))):
+        copies.append(pltpu.make_async_copy(source, target, out_sems.at[n]))
+        copies[-1].start()
     for copy in copies:
         copy.wait()
 
@@ -187,22 +203,20 @@
         pltpu.with_memory_space_constraint(x, pltpu.HBM)
         for x in (caches, queries, new_entries, lengths, targets)
     ]
-    *packs, places, att, after = pl.pallas_call(
+    *packs, places, att, stored = pl.pallas_call(
         functools.partial(attend_kernel, shifts, groups),
         out_shape=[shape((TILE + 2 * FAR, HD)), shape((TILE + CAP + NEAR, HD)), shape((CAP - NEAR, HD)),
                    shape((2 * (CAP - FAR), HD))]
         + [shape((8, HD), jnp.float32), shape((16 * REQS, HD), jnp.float32), shape(caches.shape)],
         in_specs=[HBM] * 5,
-        out_specs=[VM] * 6 + [HBM],
+        out_specs=[VM] * 7,
         scratch_shapes=[
             pltpu.SMEM(targets.shape, jnp.int32),
             pltpu.SMEM(lengths.shape, jnp.int32),
             pltpu.VMEM(queries.shape, BF),
             pltpu.VMEM(new_entries.shape, BF),
-            pltpu.VMEM(caches.shape, BF),
             pltpu.VMEM((16 * REQS, HD), jnp.float32),
             pltpu.SemaphoreType.DMA((4,)),
-            pltpu.SemaphoreType.DMA((2, REQS)),
             pltpu.SemaphoreType.DMA((2, REQS)),
         ],
         compiler_params=limit(6),
@@ -219,7 +233,6 @@
         in_specs=[VM] * 5,
         out_specs=VM,
         scratch_shapes=[
-            pltpu.VMEM((16 * REQS, HD), jnp.float32),
             pltpu.VMEM((2 * REQS, 8 * HD), BF),
         ],
         compiler_params=limit(20),
@@ -235,14 +248,16 @@
     after = pl.pallas_call(
         functools.partial(place_kernel, plan),
         out_shape=shape(caches.shape),
-        in_specs=[VM] * 3 + [HBM],
+        in_specs=[VM] * 4,
         out_specs=HBM,
-        input_output_aliases={3: 0},
-        scratch_shapes=[pltpu.SemaphoreType.DMA((sum(len(pieces) for _, pieces in plan),))],
+        scratch_shapes=[
+            pltpu.SemaphoreType.DMA((sum(len(pieces) for _, pieces in plan),)),
+            pltpu.SemaphoreType.DMA((2, REQS)),
+        ],
         compiler_params=limit(4),
         cost_estimate=pl.CostEstimate(flops=2000000000, bytes_accessed=10**6, transcendentals=0),
         name="place",
-    )(places, lead_near, lead_far, after)
+    )(places, lead_near, lead_far, stored)
 
     rest = CAP - FAR
     plan = [
@@ -253,9 +268,12 @@
         functools.partial(finish_kernel, plan),
         out_shape=[shape(caches.shape)] + [shape((REQS, width))] * 2,
         in_specs=[VM] * 3 + [HBM, VM],
-        out_specs=[HBM, VM, VM],
+        out_specs=[HBM] * 3,
         input_output_aliases={3: 0},
-        scratch_shapes=[pltpu.SemaphoreType.DMA((sum(len(pieces) for _, pieces in plan),))],
+        scratch_shapes=[pltpu.VMEM((REQS, width), BF)] * 2 + [
+            pltpu.SemaphoreType.DMA((sum(len(pieces) for _, pieces in plan),)),
+            pltpu.SemaphoreType.DMA((2,)),
+        ],
         compiler_params=limit(4),
         name="finish",
     )(places, tail_near, tail_far, after, shares)

time: 31.5 us -> 30.4 us (0.965)
  Pallas kernels: 7.05 us -> 6.24 us
    pallas_call x1, Pallas kernels: 1.47 us -> 0.89 us  [on_device(): pl.pallas_call(functools.partial(finish_kernel, plan), out_shape=[shape(c...]
    pallas_call x1, Pallas kernels: 2.48 us -> 2.14 us  [on_device(): pl.pallas_call(functools.partial(attend_kernel, shifts, groups), out_shap...]
  transfers between devices with their start and end apart: 5 -> 5, of which waited for: 3 -> 3; matrix products, arithmetic and copies ran while one was open for 0% -> 0% of each run, Pallas kernels for 10% -> 11%
where the time goes in v5:
time: 30.4 us; the launch traced here: 30.3 us
  starting transfers between devices  13.8 us (45%)
  waiting for transfers between devices  9.53 us (31%)
  Pallas kernels  6.24 us (21%)
  between operations  0.67 us (2%)
    ppermute x4, starting transfers between devices, on_device(): lax.ppermute(x, 'inst', perms[n])  9.52 us
    ppermute x4, waiting for transfers between devices, on_device(): lax.ppermute(x, 'inst', perms[n])  7.01 us
    all_to_all x1, starting transfers between devices, on_device(): shares = lax.all_to_all(partial, 'tp', 0, 0)  4.3 us
    all_to_all x1, waiting for transfers between devices, on_device(): shares = lax.all_to_all(partial, 'tp', 0, 0)  2.52 us
    pallas_call x1, Pallas kernels, on_device(): pl.pallas_call(functools.partial(attend_kernel, shifts, groups), out_shap...  2.14 us
    pallas_call x1, Pallas kernels, on_device(): pl.pallas_call(functools.partial(project_kernel, parts), out_shape=shape(...  2.12 us
    pallas_call x1, Pallas kernels, on_device(): pl.pallas_call(functools.partial(place_kernel, plan), out_shape=shape(cac...  1.08 us
    pallas_call x1, Pallas kernels, on_device(): pl.pallas_call(functools.partial(finish_kernel, plan), out_shape=[shape(c...  0.89 us
  transfers between devices with their start and end apart: 5, of which 3 were waited for; matrix products, arithmetic and copies ran while one was open for 0% of the time, Pallas kernels for 11%

profile of v5, /device:TPU:24, one launch (start us, length us, event | category | flops | bytes accessed | tf_op | source)
XLA Modules:
  0.0 30.3 jit_solution(1817425022822966887)
XLA Ops:
  0.6 0.0 copy-start
  0.6 2.1 %attend.1 = (bf16[144,128]{1,0:T(8,128)(2,1)S(1)}, bf16[656,128]{1,0:T(8,128)(2,1)S(1)}, bf16[384,128]{1,0:T(8,128)(2,1)S(1)}, bf16[896,128]{1,0:T(8,128)(2,1)S(...) custom-call(s32[128]{0:T(128)} %targets_hbm.1, s32[128]{0:T(128)} %lengths_hbm.1, ...), custom_call_target="tpu_custom_call" | custom-call | flops 10000000000 | bytes 1000000 | tf_op jit(solution)/shard_map/attend/pallas_call | solution.py:206
  2.8 1.7 %collective-permute-start.2 = (bf16[656,128]{1,0:T(8,128)(2,1)S(1)}, bf16[656,128]{1,0:T(8,128)(2,1)S(1)}, u32[]{:S(2)}, u32[]{:S(2)}) collective-permute-start(bf16[656,128]{1,0:T(8,128)(2,1)S(1)} %get-tuple-element.16), channel_id=1, source_target_pairs={{0,8},{8,16},{16,24},{24,32},{32,40},{40,48},{48,56},{56,64},{64,7... | collective-permute-start | bytes 503816 | tf_op jit(solution)/shard_map/ppermute | solution.py:227
  4.4 6.3 %collective-permute-start.3 = (bf16[144,128]{1,0:T(8,128)(2,1)S(1)}, bf16[144,128]{1,0:T(8,128)(2,1)S(1)}, u32[]{:S(2)}, u32[]{:S(2)}) collective-permute-start(bf16[144,128]{1,0:T(8,128)(2,1)S(1)} %get-tuple-element.17), channel_id=1, source_target_pairs={{0,128},{8,136},{16,144},{24,152},{32,160},{40,168},{48,176},{56,1... | collective-permute-start | bytes 110600 | tf_op jit(solution)/shard_map/ppermute | solution.py:227
  10.7 1.6 %collective-permute-start = (bf16[384,128]{1,0:T(8,128)(2,1)S(1)}, bf16[384,128]{1,0:T(8,128)(2,1)S(1)}, u32[]{:S(2)}, u32[]{:S(2)}) collective-permute-start(bf16[384,128]{1,0:T(8,128)(2,1)S(1)} %get-tuple-element.14), channel_id=1, source_target_pairs={{0,8},{8,16},{16,24},{24,32},{32,40},{40,48},{48,56},{56,64},{64,7... | collective-permute-start | bytes 294920 | tf_op jit(solution)/shard_map/ppermute | solution.py:227
  12.3 0.0 collective-permute-start.1
  12.3 4.9 %collective-permute-done.3.far_ref = bf16[144,128]{1,0:T(8,128)(2,1)S(1)} collective-permute-done((bf16[144,128]{1,0:T(8,128)(2,1)S(1)}, bf16[144,128]{1,0:T(8,128)(2,1)S(1)}, u32[]{:S(2)}, u32[]{:S(2)}) %collective-permute-start.3) | collective-permute-done | bytes 36896 | tf_op jit(solution)/shard_map/ppermute | solution.py:227
  17.2 0.0 collective-permute-done.2.near_ref
  17.2 0.0 copy-done
  17.2 2.1 %project.1 = bf16[8,8,640]{2,1,0:T(8,128)(2,1)} custom-call(f32[8,128]{1,0:T(8,128)S(1)} %get-tuple-element.13.places_ref, f32[64,128]{1,0:T(8,128)S(1)} %get-tuple-element.19.att_ref, bf16[656,128]{1,0:T(8,128)(2,1)S(1)} %collective-permute-done.2.near_ref, bf16[144,128]{1,0:T(8,128)(2,1)S(1)} %collective-permute-done.3.far_ref, bf16[1024,5120]{1,0:T(8,128)(2,1)S(1)} %copy-done), custom_call_target="tpu_custom_call" | custom-call | flops 1000000000 | bytes 1000000 | tf_op jit(solution)/shard_map/project/pallas_call | solution.py:230
  19.4 4.3 %all-to-all-start = ((bf16[8,8,640]{2,1,0:T(8,128)(2,1)}), bf16[8,8,640]{2,1,0:T(8,128)(2,1)S(1)}, u32[]{:S(2)}, u32[]{:S(2)}) async-start(bf16[8,8,640]{2,1,0:T(8,128)(2,1)} %project.1), calls=%async_computation | async-start | bytes 163840 | tf_op jit(solution)/shard_map/all_to_all | solution.py:242
  23.7 1.1 %place.1.rest_2_ = bf16[2,4,512,128]{3,2,1,0:T(8,128)(2,1)} custom-call(f32[8,128]{1,0:T(8,128)S(1)} %get-tuple-element.13.places_ref, bf16[656,128]{1,0:T(8,128)(2,1)S(1)} %collective-permute-done.2.near_ref, bf16[144,128]{1,0:T(8,128)(2,1)S(1)} %collective-permute-done.3.far_ref, bf16[2,4,512,128]{3,2,1,0:T(8,128)(2,1)S(1)} %get-tuple-element.18.stored), custom_call_target="tpu_custom_call" | custom-call | flops 2000000000 | bytes 1000000 | tf_op jit(solution)/shard_map/place/pallas_call | solution.py:248
  24.7 0.0 collective-permute-done.rest_0_
  24.8 2.1 %collective-permute-done.1.rest_1_ = bf16[896,128]{1,0:T(8,128)(2,1)S(1)} collective-permute-done((bf16[896,128]{1,0:T(8,128)(2,1)S(1)}, bf16[896,128]{1,0:T(8,128)(2,1)S(1)}, u32[]{:S(2)}, u32[]{:S(2)}) %collective-permute-start.1) | collective-permute-done | bytes 229408 | tf_op jit(solution)/shard_map/ppermute | solution.py:227
  26.9 2.5 %all-to-all-done.rest_3_ = bf16[8,8,640]{2,1,0:T(8,128)(2,1)S(1)} async-done(((bf16[8,8,640]{2,1,0:T(8,128)(2,1)}), bf16[8,8,640]{2,1,0:T(8,128)(2,1)S(1)}, u32[]{:S(2)}, u32[]{:S(2)}) %all-to-all-start) | async-done | bytes 81952 | tf_op jit(solution)/shard_map/all_to_all | solution.py:242
  29.4 0.9 %finish.1 = (bf16[2,4,512,128]{3,2,1,0:T(8,128)(2,1)}, bf16[4,640]{1,0:T(4,128)(2,1)}, bf16[4,640]{1,0:T(4,128)(2,1)}) custom-call(f32[8,128]{1,0:T(8,128)S(1)} %get-tuple-element.13.places_ref, bf16[384,128]{1,0:T(8,128)(2,1)S(1)} %collective-permute-done.rest_0_, ...), custom_call_target="tpu_custom_call", output_to_operand_aliasing={{0}: (3, {})} | custom-call | tf_op jit(solution)/shard_map/finish/pallas_call | solution.py:267
Async XLA Ops:
  0.6 16.6 %copy-start = (bf16[1024,5120]{1,0:T(8,128)(2,1)S(1)}, bf16[1024,5120]{1,0:T(8,128)(2,1)}, u32[]{:S(2)}) copy-start(bf16[1024,5120]{1,0:T(8,128)(2,1)} %weight_ref.1) | copy-start | bytes 31457284
  2.8 14.4 %collective-permute-start.2 = (bf16[656,128]{1,0:T(8,128)(2,1)S(1)}, bf16[656,128]{1,0:T(8,128)(2,1)S(1)}, u32[]{:S(2)}, u32[]{:S(2)}) collective-permute-start(bf16[656,128]{1,0:T(8,128)(2,1)S(1)} %get-tuple-element.16), channel_id=1, source_target_pairs={{0,8},{8,16},{16,24},{24,32},{32,40},{40,48},{48,56},{56,64},{64,7... | collective-permute-start | bytes 503816 | tf_op jit(solution)/shard_map/ppermute | solution.py:227
  4.4 12.8 %collective-permute-start.3 = (bf16[144,128]{1,0:T(8,128)(2,1)S(1)}, bf16[144,128]{1,0:T(8,128)(2,1)S(1)}, u32[]{:S(2)}, u32[]{:S(2)}) collective-permute-start(bf16[144,128]{1,0:T(8,128)(2,1)S(1)} %get-tuple-element.17), channel_id=1, source_target_pairs={{0,128},{8,136},{16,144},{24,152},{32,160},{40,168},{48,176},{56,1... | collective-permute-start | bytes 110600 | tf_op jit(solution)/shard_map/ppermute | solution.py:227
  10.7 14.0 %collective-permute-start = (bf16[384,128]{1,0:T(8,128)(2,1)S(1)}, bf16[384,128]{1,0:T(8,128)(2,1)S(1)}, u32[]{:S(2)}, u32[]{:S(2)}) collective-permute-start(bf16[384,128]{1,0:T(8,128)(2,1)S(1)} %get-tuple-element.14), channel_id=1, source_target_pairs={{0,8},{8,16},{16,24},{24,32},{32,40},{40,48},{48,56},{56,64},{64,7... | collective-permute-start | bytes 294920 | tf_op jit(solution)/shard_map/ppermute | solution.py:227
  12.3 14.5 %collective-permute-start.1 = (bf16[896,128]{1,0:T(8,128)(2,1)S(1)}, bf16[896,128]{1,0:T(8,128)(2,1)S(1)}, u32[]{:S(2)}, u32[]{:S(2)}) collective-permute-start(bf16[896,128]{1,0:T(8,128)(2,1)S(1)} %get-tuple-element.15), channel_id=1, source_target_pairs={{0,128},{8,136},{16,144},{24,152},{32,160},{40,168},{48,176},{56,1... | collective-permute-start | bytes 688136 | tf_op jit(solution)/shard_map/ppermute | solution.py:227
  19.4 10.0 %all-to-all-start = ((bf16[8,8,640]{2,1,0:T(8,128)(2,1)}), bf16[8,8,640]{2,1,0:T(8,128)(2,1)S(1)}, u32[]{:S(2)}, u32[]{:S(2)}) async-start(bf16[8,8,640]{2,1,0:T(8,128)(2,1)} %project.1), calls=%async_computation | async-start | bytes 163840 | tf_op jit(solution)/shard_map/all_to_all | solution.py:242

commit v6 on v5

--- a/solution.py
+++ b/solution.py
@@ -90,9 +90,9 @@
         visible = lax.broadcasted_iota(jnp.int32, scores.shape, 1) <= live
         scores = jnp.where(visible, scores, -jnp.inf)
         weights = jnp.exp(scores - jnp.max(scores, axis=-1, keepdims=True))
-        probs.append((weights / jnp.sum(weights, axis=-1, keepdims=True)).astype(BF))
+        probs.append((weights.astype(BF), jnp.sum(weights, axis=-1, keepdims=True)))
     for s in range(REQS):
-        out = jnp.dot(probs[s], stored[1, s], preferred_element_type=jnp.float32)
+        out = jnp.dot(probs[s][0], stored[1, s], preferred_element_type=jnp.float32) / probs[s][1]
         att[s * 8:(s + 1) * 8, :] = out[:8]
         att[(REQS + s) * 8:(REQS + s + 1) * 8, :] = out[8:]
     for shift, slot, lead in zip(shifts, slots, (lead_far, lead_near)):
@@ -112,8 +112,9 @@
     return jnp.max(places_ref[n:n + 1, :]).astype(jnp.int32)
 
 
-def project_kernel(parts, places_ref, att_ref, near_ref, far_ref, weight_ref, out_ref, lhs):
-    width = out_ref.shape[-1]
+def project_kernel(parts, places_ref, att_ref, near_ref, far_ref, weight_ref, mine_ref, theirs_ref, lhs):
+    width = mine_ref.shape[-1]
+    even = lax.rem(lax.axis_index("tp"), 2) == 0
     rows = lax.broadcasted_iota(jnp.int32, (2 * REQS, HD), 0).astype(jnp.float32)
     pays = [pay[:TILE, :].astype(jnp.float32) for pay in (far_ref, near_ref)]
     for h in range(8):
@@ -122,12 +123,21 @@
             at = rows == bcast_rows(places_ref[n:n + 1, :] + REQS, 2 * REQS)
             head = jnp.where(at, bcast_rows(pay[h:h + 1], 2 * REQS), head)
         lhs[:, h * HD:(h + 1) * HD] = head.astype(BF)
-    for p in range(0, parts, 2):
+    for x in range(parts // 2):
         both = jnp.dot(
-            lhs[...], weight_ref[:, p * width:(p + 2) * width], preferred_element_type=jnp.float32
-        ).astype(BF)
-        out_ref[p] = both[:, :width]
-        out_ref[p + 1] = both[:, width:]
+            lhs[...], weight_ref[:, 2 * x * width:2 * (x + 1) * width], preferred_element_type=jnp.float32
+        )
+        first, second = both[:, :width], both[:, width:]
+        mine_ref[x] = jnp.where(even, first, second)
+        theirs_ref[x] = jnp.where(even, second, first).astype(BF)
+
+
+def add_kernel(chips, mine_ref, theirs_ref, own_ref, *sends):
+    x = lax.axis_index("tp") // 2
+    own_ref[...] = mine_ref[x] + theirs_ref[x].astype(jnp.float32)
+    for d, send in enumerate(sends):
+        to = lax.rem(x + d + 1, chips)
+        send[...] = (mine_ref[to] + theirs_ref[to].astype(jnp.float32)).astype(BF)
 
 
 def start_placing(plan, places_ref, moved, after_hbm, sems):
@@ -161,9 +171,11 @@
 
 def finish_kernel(plan, places_ref, *rest):
     moved = rest[:len(plan)]
-    _, shares_ref, after_hbm, one_hbm, two_hbm, one, two, sems, out_sems = rest[len(plan):]
+    _, own_ref, *shares, after_hbm, one_hbm, two_hbm, one, two, sems, out_sems = rest[len(plan):]
     copies = start_placing(plan, places_ref, moved, after_hbm, sems)
-    total = jnp.sum(shares_ref[...].astype(jnp.float32), axis=0)
+    total = own_ref[...]
+    for share in shares:
+        total = total + share[...].astype(jnp.float32)
     one[...] = total[:REQS].astype(BF)
     two[...] = total[REQS:].astype(BF)
     for n, (source, target) in enumerate(((one, one_hbm), (two, two_hbm))):
@@ -227,19 +239,31 @@
         lax.ppermute(x, "inst", perms[n]) for x, n in zip(packs, (0, 1, 1, 0))
     ]
 
-    partial = pl.pallas_call(
+    chips = parts // 2
+    mine, theirs = pl.pallas_call(
         functools.partial(project_kernel, parts),
-        out_shape=shape((parts, 2 * REQS, width)),
+        out_shape=[shape((chips, 2 * REQS, width), jnp.float32), shape((chips, 2 * REQS, width))],
         in_specs=[VM] * 5,
-        out_specs=VM,
+        out_specs=[VM] * 2,
         scratch_shapes=[
             pltpu.VMEM((2 * REQS, 8 * HD), BF),
         ],
         compiler_params=limit(20),
-        cost_estimate=pl.CostEstimate(flops=1000000000, bytes_accessed=10**6, transcendentals=0),
+        cost_estimate=pl.CostEstimate(flops=4000000000, bytes_accessed=10**6, transcendentals=0),
         name="project",
     )(places, att, lead_near, lead_far, output_weight)
-    shares = lax.all_to_all(partial, "tp", 0, 0)
+    theirs = lax.ppermute(theirs, "tp", [(i, i + 1 - 2 * (i % 2)) for i in range(parts)])
+    own, *shares = pl.pallas_call(
+        functools.partial(add_kernel, chips),
+        out_shape=[shape((2 * REQS, width), jnp.float32)] + [shape((2 * REQS, width))] * (chips - 1),
+        in_specs=[VM] * 2,
+        out_specs=[VM] * chips,
+        compiler_params=limit(4),
+        name="add",
+    )(mine, theirs)
+    shares = [
+        lax.ppermute(x, "tp", [(i, (i + 2 * (d + 1)) % parts) for i in range(parts)]) for d, x in enumerate(shares)
+    ]
 
     plan = [
         (1, pieces_of(TILE, CAP, 0, 0, 2) + pieces_of(TILE + CAP, NEAR, 1, 0, 1)),
@@ -255,7 +279,7 @@
             pltpu.SemaphoreType.DMA((2, REQS)),
         ],
         compiler_params=limit(4),
-        cost_estimate=pl.CostEstimate(flops=2000000000, bytes_accessed=10**6, transcendentals=0),
+        cost_estimate=pl.CostEstimate(flops=500000000, bytes_accessed=10**6, transcendentals=0),
         name="place",
     )(places, lead_near, lead_far, stored)
 
@@ -267,7 +291,7 @@
     after, one, two = pl.pallas_call(
         functools.partial(finish_kernel, plan),
         out_shape=[shape(caches.shape)] + [shape((REQS, width))] * 2,
-        in_specs=[VM] * 3 + [HBM, VM],
+        in_specs=[VM] * 3 + [HBM] + [VM] * chips,
         out_specs=[HBM] * 3,
         input_output_aliases={3: 0},
         scratch_shapes=[pltpu.VMEM((REQS, width), BF)] * 2 + [
@@ -276,7 +300,7 @@
         ],
         compiler_params=limit(4),
         name="finish",
-    )(places, tail_near, tail_far, after, shares)
+    )(places, tail_near, tail_far, after, own, *shares)
     return one, two, after
 
 

time: 30.4 us -> 28.8 us (0.947)
  waiting for transfers between devices: 9.53 us -> 7.23 us
  starting transfers between devices: 13.8 us -> 15.3 us
  Pallas kernels: 6.24 us -> 5.53 us
    ppermute x0 -> x4, starting transfers between devices: none -> 5.73 us  [the longest x3 5.73 us: on_device(): lax.ppermute(x, 'tp', [(i, (i + 2 * (d + 1)) % parts) for i in range(part...]
    all_to_all x1 -> x0, starting transfers between devices: 4.3 us -> none  [on_device(): shares = lax.all_to_all(partial, 'tp', 0, 0)]
    all_to_all x1 -> x0, waiting for transfers between devices: 2.52 us -> none  [on_device(): shares = lax.all_to_all(partial, 'tp', 0, 0)]
    ppermute x0 -> x4, waiting for transfers between devices: none -> 2.34 us  [the longest x1 1.22 us: on_device(): lax.ppermute(theirs, 'tp', [(i, i + 1 - 2 * (i % 2)) for i in range(parts)])]
    ppermute x4, waiting for transfers between devices: 7.01 us -> 4.89 us  [on_device(): lax.ppermute(x, 'inst', perms[n])]
    pallas_call x1 -> x2, Pallas kernels: 2.12 us -> 1.5 us  [the longest x1 1.48 us: on_device(): pl.pallas_call(functools.partial(project_kernel, parts), out_shape=[shape...]
  transfers between devices with their start and end apart: 5 -> 8, of which waited for: 3 -> 3; matrix products, arithmetic and copies ran while one was open for 0% -> 0% of each run, Pallas kernels for 11% -> 9%
where the time goes in v6:
time: 28.8 us; the launch traced here: 28.7 us
  starting transfers between devices  15.3 us (53%)
  waiting for transfers between devices  7.23 us (25%)
  Pallas kernels  5.53 us (19%)
  between operations  0.69 us (2%)
    ppermute x4, starting transfers between devices, on_device(): lax.ppermute(x, 'inst', perms[n])  9.53 us
    ppermute x3, starting transfers between devices, on_device(): lax.ppermute(x, 'tp', [(i, (i + 2 * (d + 1)) % parts) for i in range(part...  5.73 us
    ppermute x4, waiting for transfers between devices, on_device(): lax.ppermute(x, 'inst', perms[n])  4.89 us
    pallas_call x1, Pallas kernels, on_device(): pl.pallas_call(functools.partial(attend_kernel, shifts, groups), out_shap...  2.06 us
    pallas_call x1, Pallas kernels, on_device(): pl.pallas_call(functools.partial(project_kernel, parts), out_shape=[shape...  1.48 us
    ppermute x1, waiting for transfers between devices, on_device(): lax.ppermute(theirs, 'tp', [(i, i + 1 - 2 * (i % 2)) for i in range(parts)])  1.22 us
    ppermute x3, waiting for transfers between devices, on_device(): lax.ppermute(x, 'tp', [(i, (i + 2 * (d + 1)) % parts) for i in range(part...  1.12 us
    pallas_call x1, Pallas kernels, on_device(): pl.pallas_call(functools.partial(place_kernel, plan), out_shape=shape(cac...  1.08 us
  transfers between devices with their start and end apart: 8, of which 3 were waited for; matrix products, arithmetic and copies ran while one was open for 0% of the time, Pallas kernels for 9%

profile of v6, /device:TPU:24, one launch (start us, length us, event | category | flops | bytes accessed | tf_op | source)
XLA Modules:
  0.0 28.7 jit_solution(3142043968764510950)
XLA Ops:
  0.6 0.0 copy-start
  0.6 2.1 %attend.1 = (bf16[144,128]{1,0:T(8,128)(2,1)S(1)}, bf16[656,128]{1,0:T(8,128)(2,1)S(1)}, bf16[384,128]{1,0:T(8,128)(2,1)S(1)}, bf16[896,128]{1,0:T(8,128)(2,1)S(...) custom-call(s32[128]{0:T(128)} %targets_hbm.1, s32[128]{0:T(128)} %lengths_hbm.1, ...), custom_call_target="tpu_custom_call" | custom-call | flops 10000000000 | bytes 1000000 | tf_op jit(solution)/shard_map/attend/pallas_call | solution.py:218
  2.7 1.7 %collective-permute-start.2 = (bf16[656,128]{1,0:T(8,128)(2,1)S(1)}, bf16[656,128]{1,0:T(8,128)(2,1)S(1)}, u32[]{:S(2)}, u32[]{:S(2)}) collective-permute-start(bf16[656,128]{1,0:T(8,128)(2,1)S(1)} %get-tuple-element.22), channel_id=1, source_target_pairs={{0,8},{8,16},{16,24},{24,32},{32,40},{40,48},{48,56},{56,64},{64,7... | collective-permute-start | bytes 503816 | tf_op jit(solution)/shard_map/ppermute | solution.py:239
  4.4 6.3 %collective-permute-start.3 = (bf16[144,128]{1,0:T(8,128)(2,1)S(1)}, bf16[144,128]{1,0:T(8,128)(2,1)S(1)}, u32[]{:S(2)}, u32[]{:S(2)}) collective-permute-start(bf16[144,128]{1,0:T(8,128)(2,1)S(1)} %get-tuple-element.23), channel_id=1, source_target_pairs={{0,128},{8,136},{16,144},{24,152},{32,160},{40,168},{48,176},{56,1... | collective-permute-start | bytes 110600 | tf_op jit(solution)/shard_map/ppermute | solution.py:239
  10.7 1.6 %collective-permute-start = (bf16[384,128]{1,0:T(8,128)(2,1)S(1)}, bf16[384,128]{1,0:T(8,128)(2,1)S(1)}, u32[]{:S(2)}, u32[]{:S(2)}) collective-permute-start(bf16[384,128]{1,0:T(8,128)(2,1)S(1)} %get-tuple-element.20), channel_id=1, source_target_pairs={{0,8},{8,16},{16,24},{24,32},{32,40},{40,48},{48,56},{56,64},{64,7... | collective-permute-start | bytes 294920 | tf_op jit(solution)/shard_map/ppermute | solution.py:239
  12.2 0.0 collective-permute-start.1
  12.2 4.9 %collective-permute-done.3.far_ref = bf16[144,128]{1,0:T(8,128)(2,1)S(1)} collective-permute-done((bf16[144,128]{1,0:T(8,128)(2,1)S(1)}, bf16[144,128]{1,0:T(8,128)(2,1)S(1)}, u32[]{:S(2)}, u32[]{:S(2)}) %collective-permute-start.3) | collective-permute-done | bytes 36896 | tf_op jit(solution)/shard_map/ppermute | solution.py:239
  17.1 0.0 collective-permute-done.2.near_ref
  17.1 0.0 copy-done
  17.1 1.5 %project.1 = (f32[4,8,640]{2,1,0:T(8,128)S(1)}, bf16[4,8,640]{2,1,0:T(8,128)(2,1)S(1)}) custom-call(f32[8,128]{1,0:T(8,128)S(1)} %get-tuple-element.19.places_ref, f32[64,128]{1,0:T(8,128)S(1)} %get-tuple-element.25.att_ref, bf16[656,128]{1,0:T(8,128)(2,1)S(1)} %collective-permute-done.2.near_ref, bf16[144,128]{1,0:T(8,128)(2,1)S(1)} %collective-permute-done.3.far_ref, ...), custom_call_target="tpu_custom_call" | custom-call | flops 4000000000 | bytes 1000000 | tf_op jit(solution)/shard_map/project/pallas_call | solution.py:243
  18.6 0.0 collective-permute-start.4
  18.6 1.2 %collective-permute-done.4.theirs_ref = bf16[4,8,640]{2,1,0:T(8,128)(2,1)S(1)} collective-permute-done((bf16[4,8,640]{2,1,0:T(8,128)(2,1)S(1)}, bf16[4,8,640]{2,1,0:T(8,128)(2,1)S(1)}, u32[]{:S(2)}, u32[]{:S(2)}) %collective-permute-start.4) | collective-permute-done | bytes 40992 | tf_op jit(solution)/shard_map/ppermute | solution.py:255
  19.8 1.6 %collective-permute-start.5 = (bf16[8,640]{1,0:T(8,128)(2,1)S(1)}, bf16[8,640]{1,0:T(8,128)(2,1)S(1)}, u32[]{:S(2)}, u32[]{:S(2)}) collective-permute-start(bf16[8,640]{1,0:T(8,128)(2,1)S(1)} %get-tuple-element.29), channel_id=1, source_target_pairs={{0,2},{1,3},{2,4},{3,5},{4,6},{5,7},{6,0},{7,1},{8,10},{9,11},{10,... | collective-permute-start | bytes 30728 | tf_op jit(solution)/shard_map/ppermute | solution.py:265
  21.4 2.7 %collective-permute-start.6 = (bf16[8,640]{1,0:T(8,128)(2,1)S(1)}, bf16[8,640]{1,0:T(8,128)(2,1)S(1)}, u32[]{:S(2)}, u32[]{:S(2)}) collective-permute-start(bf16[8,640]{1,0:T(8,128)(2,1)S(1)} %get-tuple-element.30), channel_id=1, source_target_pairs={{0,4},{1,5},{2,6},{3,7},{4,0},{5,1},{6,2},{7,3},{8,12},{9,13},{10,... | collective-permute-start | bytes 30728 | tf_op jit(solution)/shard_map/ppermute | solution.py:265
  24.1 1.4 %collective-permute-start.7 = (bf16[8,640]{1,0:T(8,128)(2,1)S(1)}, bf16[8,640]{1,0:T(8,128)(2,1)S(1)}, u32[]{:S(2)}, u32[]{:S(2)}) collective-permute-start(bf16[8,640]{1,0:T(8,128)(2,1)S(1)} %get-tuple-element.31), channel_id=1, source_target_pairs={{0,6},{1,7},{2,0},{3,1},{4,2},{5,3},{6,4},{7,5},{8,14},{9,15},{10,... | collective-permute-start | bytes 30728 | tf_op jit(solution)/shard_map/ppermute | solution.py:265
  25.6 1.1 %place.1.rest_2_ = bf16[2,4,512,128]{3,2,1,0:T(8,128)(2,1)} custom-call(f32[8,128]{1,0:T(8,128)S(1)} %get-tuple-element.19.places_ref, bf16[656,128]{1,0:T(8,128)(2,1)S(1)} %collective-permute-done.2.near_ref, bf16[144,128]{1,0:T(8,128)(2,1)S(1)} %collective-permute-done.3.far_ref, bf16[2,4,512,128]{3,2,1,0:T(8,128)(2,1)S(1)} %get-tuple-element.24.stored), custom_call_target="tpu_custom_call" | custom-call | flops 500000000 | bytes 1000000 | tf_op jit(solution)/shard_map/place/pallas_call | solution.py:272
  26.7 0.0 collective-permute-done.rest_0_
  26.7 0.0 collective-permute-done.5.rest_4_
  26.7 0.0 collective-permute-done.6.rest_5_
  26.7 1.1 %collective-permute-done.7.rest_6_ = bf16[8,640]{1,0:T(8,128)(2,1)S(1)} collective-permute-done((bf16[8,640]{1,0:T(8,128)(2,1)S(1)}, bf16[8,640]{1,0:T(8,128)(2,1)S(1)}, u32[]{:S(2)}, u32[]{:S(2)}) %collective-permute-start.7) | collective-permute-done | bytes 10272 | tf_op jit(solution)/shard_map/ppermute | solution.py:265
  27.8 0.0 collective-permute-done.1.rest_1_
  27.8 0.9 %finish.1 = (bf16[2,4,512,128]{3,2,1,0:T(8,128)(2,1)}, bf16[4,640]{1,0:T(4,128)(2,1)}, bf16[4,640]{1,0:T(4,128)(2,1)}) custom-call(f32[8,128]{1,0:T(8,128)S(1)} %get-tuple-element.19.places_ref, bf16[384,128]{1,0:T(8,128)(2,1)S(1)} %collective-permute-done.rest_0_, ...), custom_call_target="tpu_custom_call", output_to_operand_aliasing={{0}: (3, {})} | custom-call | tf_op jit(solution)/shard_map/finish/pallas_call | solution.py:291
  (1 shorter events, 0.0 us)
Async XLA Ops:
  0.6 16.5 %copy-start = (bf16[1024,5120]{1,0:T(8,128)(2,1)S(1)}, bf16[1024,5120]{1,0:T(8,128)(2,1)}, u32[]{:S(2)}) copy-start(bf16[1024,5120]{1,0:T(8,128)(2,1)} %weight_ref.1) | copy-start | bytes 31457284
  2.7 14.4 %collective-permute-start.2 = (bf16[656,128]{1,0:T(8,128)(2,1)S(1)}, bf16[656,128]{1,0:T(8,128)(2,1)S(1)}, u32[]{:S(2)}, u32[]{:S(2)}) collective-permute-start(bf16[656,128]{1,0:T(8,128)(2,1)S(1)} %get-tuple-element.22), channel_id=1, source_target_pairs={{0,8},{8,16},{16,24},{24,32},{32,40},{40,48},{48,56},{56,64},{64,7... | collective-permute-start | bytes 503816 | tf_op jit(solution)/shard_map/ppermute | solution.py:239
  4.4 12.8 %collective-permute-start.3 = (bf16[144,128]{1,0:T(8,128)(2,1)S(1)}, bf16[144,128]{1,0:T(8,128)(2,1)S(1)}, u32[]{:S(2)}, u32[]{:S(2)}) collective-permute-start(bf16[144,128]{1,0:T(8,128)(2,1)S(1)} %get-tuple-element.23), channel_id=1, source_target_pairs={{0,128},{8,136},{16,144},{24,152},{32,160},{40,168},{48,176},{56,1... | collective-permute-start | bytes 110600 | tf_op jit(solution)/shard_map/ppermute | solution.py:239
  10.7 16.0 %collective-permute-start = (bf16[384,128]{1,0:T(8,128)(2,1)S(1)}, bf16[384,128]{1,0:T(8,128)(2,1)S(1)}, u32[]{:S(2)}, u32[]{:S(2)}) collective-permute-start(bf16[384,128]{1,0:T(8,128)(2,1)S(1)} %get-tuple-element.20), channel_id=1, source_target_pairs={{0,8},{8,16},{16,24},{24,32},{32,40},{40,48},{48,56},{56,64},{64,7... | collective-permute-start | bytes 294920 | tf_op jit(solution)/shard_map/ppermute | solution.py:239
  12.2 15.6 %collective-permute-start.1 = (bf16[896,128]{1,0:T(8,128)(2,1)S(1)}, bf16[896,128]{1,0:T(8,128)(2,1)S(1)}, u32[]{:S(2)}, u32[]{:S(2)}) collective-permute-start(bf16[896,128]{1,0:T(8,128)(2,1)S(1)} %get-tuple-element.21), channel_id=1, source_target_pairs={{0,128},{8,136},{16,144},{24,152},{32,160},{40,168},{48,176},{56,1... | collective-permute-start | bytes 688136 | tf_op jit(solution)/shard_map/ppermute | solution.py:239
  18.6 1.2 %collective-permute-start.4 = (bf16[4,8,640]{2,1,0:T(8,128)(2,1)S(1)}, bf16[4,8,640]{2,1,0:T(8,128)(2,1)S(1)}, u32[]{:S(2)}, u32[]{:S(2)}) collective-permute-start(bf16[4,8,640]{2,1,0:T(8,128)(2,1)S(1)} %get-tuple-element.27), channel_id=1, source_target_pairs={{0,1},{1,0},{2,3},{3,2},{4,5},{5,4},{6,7},{7,6},{8,9},{9,8},{10,11... | collective-permute-start | bytes 122888 | tf_op jit(solution)/shard_map/ppermute | solution.py:255
  19.8 6.8 %collective-permute-start.5 = (bf16[8,640]{1,0:T(8,128)(2,1)S(1)}, bf16[8,640]{1,0:T(8,128)(2,1)S(1)}, u32[]{:S(2)}, u32[]{:S(2)}) collective-permute-start(bf16[8,640]{1,0:T(8,128)(2,1)S(1)} %get-tuple-element.29), channel_id=1, source_target_pairs={{0,2},{1,3},{2,4},{3,5},{4,6},{5,7},{6,0},{7,1},{8,10},{9,11},{10,... | collective-permute-start | bytes 30728 | tf_op jit(solution)/shard_map/ppermute | solution.py:265
  21.4 5.3 %collective-permute-start.6 = (bf16[8,640]{1,0:T(8,128)(2,1)S(1)}, bf16[8,640]{1,0:T(8,128)(2,1)S(1)}, u32[]{:S(2)}, u32[]{:S(2)}) collective-permute-start(bf16[8,640]{1,0:T(8,128)(2,1)S(1)} %get-tuple-element.30), channel_id=1, source_target_pairs={{0,4},{1,5},{2,6},{3,7},{4,0},{5,1},{6,2},{7,3},{8,12},{9,13},{10,... | collective-permute-start | bytes 30728 | tf_op jit(solution)/shard_map/ppermute | solution.py:265
  24.1 3.7 %collective-permute-start.7 = (bf16[8,640]{1,0:T(8,128)(2,1)S(1)}, bf16[8,640]{1,0:T(8,128)(2,1)S(1)}, u32[]{:S(2)}, u32[]{:S(2)}) collective-permute-start(bf16[8,640]{1,0:T(8,128)(2,1)S(1)} %get-tuple-element.31), channel_id=1, source_target_pairs={{0,6},{1,7},{2,0},{3,1},{4,2},{5,3},{6,4},{7,5},{8,14},{9,15},{10,... | collective-permute-start | bytes 30728 | tf_op jit(solution)/shard_map/ppermute | solution.py:265

commit v7 on v6

--- a/solution.py
+++ b/solution.py
@@ -112,9 +112,7 @@
     return jnp.max(places_ref[n:n + 1, :]).astype(jnp.int32)
 
 
-def project_kernel(parts, places_ref, att_ref, near_ref, far_ref, weight_ref, mine_ref, theirs_ref, lhs):
-    width = mine_ref.shape[-1]
-    even = lax.rem(lax.axis_index("tp"), 2) == 0
+def project_kernel(places_ref, att_ref, near_ref, far_ref, weight_ref, theirs_ref, lhs):
     rows = lax.broadcasted_iota(jnp.int32, (2 * REQS, HD), 0).astype(jnp.float32)
     pays = [pay[:TILE, :].astype(jnp.float32) for pay in (far_ref, near_ref)]
     for h in range(8):
@@ -123,13 +121,21 @@
             at = rows == bcast_rows(places_ref[n:n + 1, :] + REQS, 2 * REQS)
             head = jnp.where(at, bcast_rows(pay[h:h + 1], 2 * REQS), head)
         lhs[:, h * HD:(h + 1) * HD] = head.astype(BF)
-    for x in range(parts // 2):
-        both = jnp.dot(
-            lhs[...], weight_ref[:, 2 * x * width:2 * (x + 1) * width], preferred_element_type=jnp.float32
-        )
-        first, second = both[:, :width], both[:, width:]
-        mine_ref[x] = jnp.where(even, first, second)
-        theirs_ref[x] = jnp.where(even, second, first).astype(BF)
+    project_half(lhs, weight_ref, 1, theirs_ref)
+
+
+def project_half(lhs, weight_ref, other, out_ref):
+    width = out_ref.shape[-1]
+    core = lax.rem(lax.axis_index("tp") + other, 2)
+    for x in range(out_ref.shape[0]):
+        first = pl.multiple_of((2 * x + core) * width, HD)
+        out_ref[x] = jnp.dot(
+            lhs[...], weight_ref[:, pl.ds(first, width)], preferred_element_type=jnp.float32
+        ).astype(out_ref.dtype)
+
+
+def own_kernel(lhs, weight_ref, mine_ref):
+    project_half(lhs, weight_ref, 0, mine_ref)
 
 
 def add_kernel(chips, mine_ref, theirs_ref, own_ref, *sends):
@@ -240,18 +246,24 @@
     ]
 
     chips = parts // 2
-    mine, theirs = pl.pallas_call(
-        functools.partial(project_kernel, parts),
-        out_shape=[shape((chips, 2 * REQS, width), jnp.float32), shape((chips, 2 * REQS, width))],
+    theirs, lhs = pl.pallas_call(
+        project_kernel,
+        out_shape=[shape((chips, 2 * REQS, width)), shape((2 * REQS, 8 * HD))],
         in_specs=[VM] * 5,
         out_specs=[VM] * 2,
-        scratch_shapes=[
-            pltpu.VMEM((2 * REQS, 8 * HD), BF),
-        ],
         compiler_params=limit(20),
         cost_estimate=pl.CostEstimate(flops=4000000000, bytes_accessed=10**6, transcendentals=0),
         name="project",
     )(places, att, lead_near, lead_far, output_weight)
+    mine = pl.pallas_call(
+        own_kernel,
+        out_shape=shape((chips, 2 * REQS, width), jnp.float32),
+        in_specs=[VM] * 2,
+        out_specs=VM,
+        compiler_params=limit(20),
+        cost_estimate=pl.CostEstimate(flops=10**9, bytes_accessed=10**6, transcendentals=0),
+        name="own",
+    )(lhs, output_weight)
     theirs = lax.ppermute(theirs, "tp", [(i, i + 1 - 2 * (i % 2)) for i in range(parts)])
     own, *shares = pl.pallas_call(
         functools.partial(add_kernel, chips),

time: 28.8 us -> 28.5 us (0.990)
  waiting for transfers between devices: 7.23 us -> 6.35 us
    ppermute x1, waiting for transfers between devices: 1.22 us -> 0.35 us  [on_device(): lax.ppermute(theirs, 'tp', [(i, i + 1 - 2 * (i % 2)) for i in range(parts)])]
    pallas_call x1 -> x2, Pallas kernels: 1.48 us -> 1.72 us  [the longest x1 0.86 us: on_device(): pl.pallas_call(project_kernel, out_shape=[shape((chips, 2 * REQS, width))...]
  transfers between devices with their start and end apart: 8 -> 8, of which waited for: 3 -> 3; matrix products, arithmetic and copies ran while one was open for 0% -> 0% of each run, Pallas kernels for 9% -> 10%
where the time goes in v7:
time: 28.5 us; the launch traced here: 28.2 us
  starting transfers between devices  15.3 us (54%)
  waiting for transfers between devices  6.35 us (22%)
  Pallas kernels  5.77 us (20%)
  between operations  0.7 us (2%)
    ppermute x4, starting transfers between devices, on_device(): lax.ppermute(x, 'inst', perms[n])  9.53 us
    ppermute x3, starting transfers between devices, on_device(): lax.ppermute(x, 'tp', [(i, (i + 2 * (d + 1)) % parts) for i in range(part...  5.73 us
    ppermute x4, waiting for transfers between devices, on_device(): lax.ppermute(x, 'inst', perms[n])  4.88 us
    pallas_call x1, Pallas kernels, on_device(): pl.pallas_call(functools.partial(attend_kernel, shifts, groups), out_shap...  2.06 us
    ppermute x3, waiting for transfers between devices, on_device(): lax.ppermute(x, 'tp', [(i, (i + 2 * (d + 1)) % parts) for i in range(part...  1.12 us
    pallas_call x1, Pallas kernels, on_device(): pl.pallas_call(functools.partial(place_kernel, plan), out_shape=shape(cac...  1.08 us
    pallas_call x1, Pallas kernels, on_device(): pl.pallas_call(functools.partial(finish_kernel, plan), out_shape=[shape(c...  0.9 us
    pallas_call x1, Pallas kernels, on_device(): pl.pallas_call(project_kernel, out_shape=[shape((chips, 2 * REQS, width))...  0.86 us
  transfers between devices with their start and end apart: 8, of which 3 were waited for; matrix products, arithmetic and copies ran while one was open for 0% of the time, Pallas kernels for 10%

profile of v7, /device:TPU:24, one launch (start us, length us, event | category | flops | bytes accessed | tf_op | source)
XLA Modules:
  0.0 28.2 jit_solution(13390173707293676525)
XLA Ops:
  0.6 0.0 copy-start
  0.6 2.1 %attend.1 = (bf16[144,128]{1,0:T(8,128)(2,1)S(1)}, bf16[656,128]{1,0:T(8,128)(2,1)S(1)}, bf16[384,128]{1,0:T(8,128)(2,1)S(1)}, bf16[896,128]{1,0:T(8,128)(2,1)S(...) custom-call(s32[128]{0:T(128)} %targets_hbm.1, s32[128]{0:T(128)} %lengths_hbm.1, ...), custom_call_target="tpu_custom_call" | custom-call | flops 10000000000 | bytes 1000000 | tf_op jit(solution)/shard_map/attend/pallas_call | solution.py:224
  2.7 1.7 %collective-permute-start.2 = (bf16[656,128]{1,0:T(8,128)(2,1)S(1)}, bf16[656,128]{1,0:T(8,128)(2,1)S(1)}, u32[]{:S(2)}, u32[]{:S(2)}) collective-permute-start(bf16[656,128]{1,0:T(8,128)(2,1)S(1)} %get-tuple-element.22), channel_id=1, source_target_pairs={{0,8},{8,16},{16,24},{24,32},{32,40},{40,48},{48,56},{56,64},{64,7... | collective-permute-start | bytes 503816 | tf_op jit(solution)/shard_map/ppermute | solution.py:245
  4.4 6.3 %collective-permute-start.3 = (bf16[144,128]{1,0:T(8,128)(2,1)S(1)}, bf16[144,128]{1,0:T(8,128)(2,1)S(1)}, u32[]{:S(2)}, u32[]{:S(2)}) collective-permute-start(bf16[144,128]{1,0:T(8,128)(2,1)S(1)} %get-tuple-element.23), channel_id=1, source_target_pairs={{0,128},{8,136},{16,144},{24,152},{32,160},{40,168},{48,176},{56,1... | collective-permute-start | bytes 110600 | tf_op jit(solution)/shard_map/ppermute | solution.py:245
  10.7 1.6 %collective-permute-start = (bf16[384,128]{1,0:T(8,128)(2,1)S(1)}, bf16[384,128]{1,0:T(8,128)(2,1)S(1)}, u32[]{:S(2)}, u32[]{:S(2)}) collective-permute-start(bf16[384,128]{1,0:T(8,128)(2,1)S(1)} %get-tuple-element.20), channel_id=1, source_target_pairs={{0,8},{8,16},{16,24},{24,32},{32,40},{40,48},{48,56},{56,64},{64,7... | collective-permute-start | bytes 294920 | tf_op jit(solution)/shard_map/ppermute | solution.py:245
  12.2 0.0 collective-permute-start.1
  12.2 4.9 %collective-permute-done.3.far_ref = bf16[144,128]{1,0:T(8,128)(2,1)S(1)} collective-permute-done((bf16[144,128]{1,0:T(8,128)(2,1)S(1)}, bf16[144,128]{1,0:T(8,128)(2,1)S(1)}, u32[]{:S(2)}, u32[]{:S(2)}) %collective-permute-start.3) | collective-permute-done | bytes 36896 | tf_op jit(solution)/shard_map/ppermute | solution.py:245
  17.1 0.0 collective-permute-done.2.near_ref
  17.1 0.0 copy-done
  17.1 0.9 %project.1 = (bf16[4,8,640]{2,1,0:T(8,128)(2,1)S(1)}, bf16[8,1024]{1,0:T(8,128)(2,1)S(1)}) custom-call(f32[8,128]{1,0:T(8,128)S(1)} %get-tuple-element.19.places_ref, f32[64,128]{1,0:T(8,128)S(1)} %get-tuple-element.25.att_ref, bf16[656,128]{1,0:T(8,128)(2,1)S(1)} %collective-permute-done.2.near_ref, bf16[144,128]{1,0:T(8,128)(2,1)S(1)} %collective-permute-done.3.far_ref, ...), custom_call_target="tpu_custom_call" | custom-call | flops 4000000000 | bytes 1000000 | tf_op jit(solution)/shard_map/project/pallas_call | solution.py:249
  18.0 0.1 collective-permute-start.4
  18.1 0.9 %own.1.mine_ref = f32[4,8,640]{2,1,0:T(8,128)S(1)} custom-call(bf16[8,1024]{1,0:T(8,128)(2,1)S(1)} %get-tuple-element.26.lhs, bf16[1024,5120]{1,0:T(8,128)(2,1)S(1)} %copy-done), custom_call_target="tpu_custom_call" | custom-call | flops 1000000000 | bytes 1000000 | tf_op jit(solution)/shard_map/own/pallas_call | solution.py:258
  18.9 0.3 %collective-permute-done.4.theirs_ref = bf16[4,8,640]{2,1,0:T(8,128)(2,1)S(1)} collective-permute-done((bf16[4,8,640]{2,1,0:T(8,128)(2,1)S(1)}, bf16[4,8,640]{2,1,0:T(8,128)(2,1)S(1)}, u32[]{:S(2)}, u32[]{:S(2)}) %collective-permute-start.4) | collective-permute-done | bytes 40992 | tf_op jit(solution)/shard_map/ppermute | solution.py:267
  19.3 1.6 %collective-permute-start.5 = (bf16[8,640]{1,0:T(8,128)(2,1)S(1)}, bf16[8,640]{1,0:T(8,128)(2,1)S(1)}, u32[]{:S(2)}, u32[]{:S(2)}) collective-permute-start(bf16[8,640]{1,0:T(8,128)(2,1)S(1)} %get-tuple-element.29), channel_id=1, source_target_pairs={{0,2},{1,3},{2,4},{3,5},{4,6},{5,7},{6,0},{7,1},{8,10},{9,11},{10,... | collective-permute-start | bytes 30728 | tf_op jit(solution)/shard_map/ppermute | solution.py:277
  20.9 2.7 %collective-permute-start.6 = (bf16[8,640]{1,0:T(8,128)(2,1)S(1)}, bf16[8,640]{1,0:T(8,128)(2,1)S(1)}, u32[]{:S(2)}, u32[]{:S(2)}) collective-permute-start(bf16[8,640]{1,0:T(8,128)(2,1)S(1)} %get-tuple-element.30), channel_id=1, source_target_pairs={{0,4},{1,5},{2,6},{3,7},{4,0},{5,1},{6,2},{7,3},{8,12},{9,13},{10,... | collective-permute-start | bytes 30728 | tf_op jit(solution)/shard_map/ppermute | solution.py:277
  23.6 1.4 %collective-permute-start.7 = (bf16[8,640]{1,0:T(8,128)(2,1)S(1)}, bf16[8,640]{1,0:T(8,128)(2,1)S(1)}, u32[]{:S(2)}, u32[]{:S(2)}) collective-permute-start(bf16[8,640]{1,0:T(8,128)(2,1)S(1)} %get-tuple-element.31), channel_id=1, source_target_pairs={{0,6},{1,7},{2,0},{3,1},{4,2},{5,3},{6,4},{7,5},{8,14},{9,15},{10,... | collective-permute-start | bytes 30728 | tf_op jit(solution)/shard_map/ppermute | solution.py:277
  25.0 1.1 %place.1.rest_2_ = bf16[2,4,512,128]{3,2,1,0:T(8,128)(2,1)} custom-call(f32[8,128]{1,0:T(8,128)S(1)} %get-tuple-element.19.places_ref, bf16[656,128]{1,0:T(8,128)(2,1)S(1)} %collective-permute-done.2.near_ref, bf16[144,128]{1,0:T(8,128)(2,1)S(1)} %collective-permute-done.3.far_ref, bf16[2,4,512,128]{3,2,1,0:T(8,128)(2,1)S(1)} %get-tuple-element.24.stored), custom_call_target="tpu_custom_call" | custom-call | flops 500000000 | bytes 1000000 | tf_op jit(solution)/shard_map/place/pallas_call | solution.py:284
  26.1 0.0 collective-permute-done.rest_0_
  26.1 0.0 collective-permute-done.5.rest_4_
  26.1 0.0 collective-permute-done.6.rest_5_
  26.1 1.1 %collective-permute-done.7.rest_6_ = bf16[8,640]{1,0:T(8,128)(2,1)S(1)} collective-permute-done((bf16[8,640]{1,0:T(8,128)(2,1)S(1)}, bf16[8,640]{1,0:T(8,128)(2,1)S(1)}, u32[]{:S(2)}, u32[]{:S(2)}) %collective-permute-start.7) | collective-permute-done | bytes 10272 | tf_op jit(solution)/shard_map/ppermute | solution.py:277
  27.3 0.0 collective-permute-done.1.rest_1_
  27.3 0.9 %finish.1 = (bf16[2,4,512,128]{3,2,1,0:T(8,128)(2,1)}, bf16[4,640]{1,0:T(4,128)(2,1)}, bf16[4,640]{1,0:T(4,128)(2,1)}) custom-call(f32[8,128]{1,0:T(8,128)S(1)} %get-tuple-element.19.places_ref, bf16[384,128]{1,0:T(8,128)(2,1)S(1)} %collective-permute-done.rest_0_, ...), custom_call_target="tpu_custom_call", output_to_operand_aliasing={{0}: (3, {})} | custom-call | tf_op jit(solution)/shard_map/finish/pallas_call | solution.py:303
  (1 shorter events, 0.0 us)
Async XLA Ops:
  0.6 16.5 %copy-start = (bf16[1024,5120]{1,0:T(8,128)(2,1)S(1)}, bf16[1024,5120]{1,0:T(8,128)(2,1)}, u32[]{:S(2)}) copy-start(bf16[1024,5120]{1,0:T(8,128)(2,1)} %weight_ref.3) | copy-start | bytes 31457284
  2.7 14.4 %collective-permute-start.2 = (bf16[656,128]{1,0:T(8,128)(2,1)S(1)}, bf16[656,128]{1,0:T(8,128)(2,1)S(1)}, u32[]{:S(2)}, u32[]{:S(2)}) collective-permute-start(bf16[656,128]{1,0:T(8,128)(2,1)S(1)} %get-tuple-element.22), channel_id=1, source_target_pairs={{0,8},{8,16},{16,24},{24,32},{32,40},{40,48},{48,56},{56,64},{64,7... | collective-permute-start | bytes 503816 | tf_op jit(solution)/shard_map/ppermute | solution.py:245
  4.4 12.7 %collective-permute-start.3 = (bf16[144,128]{1,0:T(8,128)(2,1)S(1)}, bf16[144,128]{1,0:T(8,128)(2,1)S(1)}, u32[]{:S(2)}, u32[]{:S(2)}) collective-permute-start(bf16[144,128]{1,0:T(8,128)(2,1)S(1)} %get-tuple-element.23), channel_id=1, source_target_pairs={{0,128},{8,136},{16,144},{24,152},{32,160},{40,168},{48,176},{56,1... | collective-permute-start | bytes 110600 | tf_op jit(solution)/shard_map/ppermute | solution.py:245
  10.7 15.5 %collective-permute-start = (bf16[384,128]{1,0:T(8,128)(2,1)S(1)}, bf16[384,128]{1,0:T(8,128)(2,1)S(1)}, u32[]{:S(2)}, u32[]{:S(2)}) collective-permute-start(bf16[384,128]{1,0:T(8,128)(2,1)S(1)} %get-tuple-element.20), channel_id=1, source_target_pairs={{0,8},{8,16},{16,24},{24,32},{32,40},{40,48},{48,56},{56,64},{64,7... | collective-permute-start | bytes 294920 | tf_op jit(solution)/shard_map/ppermute | solution.py:245
  12.2 15.0 %collective-permute-start.1 = (bf16[896,128]{1,0:T(8,128)(2,1)S(1)}, bf16[896,128]{1,0:T(8,128)(2,1)S(1)}, u32[]{:S(2)}, u32[]{:S(2)}) collective-permute-start(bf16[896,128]{1,0:T(8,128)(2,1)S(1)} %get-tuple-element.21), channel_id=1, source_target_pairs={{0,128},{8,136},{16,144},{24,152},{32,160},{40,168},{48,176},{56,1... | collective-permute-start | bytes 688136 | tf_op jit(solution)/shard_map/ppermute | solution.py:245
  18.0 1.3 %collective-permute-start.4 = (bf16[4,8,640]{2,1,0:T(8,128)(2,1)S(1)}, bf16[4,8,640]{2,1,0:T(8,128)(2,1)S(1)}, u32[]{:S(2)}, u32[]{:S(2)}) collective-permute-start(bf16[4,8,640]{2,1,0:T(8,128)(2,1)S(1)} %get-tuple-element.27), channel_id=1, source_target_pairs={{0,1},{1,0},{2,3},{3,2},{4,5},{5,4},{6,7},{7,6},{8,9},{9,8},{10,11... | collective-permute-start | bytes 122888 | tf_op jit(solution)/shard_map/ppermute | solution.py:267
  19.3 6.8 %collective-permute-start.5 = (bf16[8,640]{1,0:T(8,128)(2,1)S(1)}, bf16[8,640]{1,0:T(8,128)(2,1)S(1)}, u32[]{:S(2)}, u32[]{:S(2)}) collective-permute-start(bf16[8,640]{1,0:T(8,128)(2,1)S(1)} %get-tuple-element.29), channel_id=1, source_target_pairs={{0,2},{1,3},{2,4},{3,5},{4,6},{5,7},{6,0},{7,1},{8,10},{9,11},{10,... | collective-permute-start | bytes 30728 | tf_op jit(solution)/shard_map/ppermute | solution.py:277
  20.9 5.3 %collective-permute-start.6 = (bf16[8,640]{1,0:T(8,128)(2,1)S(1)}, bf16[8,640]{1,0:T(8,128)(2,1)S(1)}, u32[]{:S(2)}, u32[]{:S(2)}) collective-permute-start(bf16[8,640]{1,0:T(8,128)(2,1)S(1)} %get-tuple-element.30), channel_id=1, source_target_pairs={{0,4},{1,5},{2,6},{3,7},{4,0},{5,1},{6,2},{7,3},{8,12},{9,13},{10,... | collective-permute-start | bytes 30728 | tf_op jit(solution)/shard_map/ppermute | solution.py:277
  23.6 3.7 %collective-permute-start.7 = (bf16[8,640]{1,0:T(8,128)(2,1)S(1)}, bf16[8,640]{1,0:T(8,128)(2,1)S(1)}, u32[]{:S(2)}, u32[]{:S(2)}) collective-permute-start(bf16[8,640]{1,0:T(8,128)(2,1)S(1)} %get-tuple-element.31), channel_id=1, source_target_pairs={{0,6},{1,7},{2,0},{3,1},{4,2},{5,3},{6,4},{7,5},{8,14},{9,15},{10,... | collective-permute-start | bytes 30728 | tf_op jit(solution)/shard_map/ppermute | solution.py:277

commit v8 on v7

--- a/solution.py
+++ b/solution.py
@@ -109,7 +109,7 @@
 
 
 def place_of(places_ref, n):
-    return jnp.max(places_ref[n:n + 1, :]).astype(jnp.int32)
+    return places_ref[n, 0].astype(jnp.int32)
 
 
 def project_kernel(places_ref, att_ref, near_ref, far_ref, weight_ref, theirs_ref, lhs):

time: 28.5 us -> 28.5 us (level)
  no operation moved by 1% of the time
where the time goes in v8:
time: 28.5 us; the launch traced here: 28.1 us
  starting transfers between devices  15.3 us (54%)
  waiting for transfers between devices  6.44 us (23%)
  Pallas kernels  5.61 us (20%)
  between operations  0.7 us (2%)
    ppermute x4, starting transfers between devices, on_device(): lax.ppermute(x, 'inst', perms[n])  9.53 us
    ppermute x3, starting transfers between devices, on_device(): lax.ppermute(x, 'tp', [(i, (i + 2 * (d + 1)) % parts) for i in range(part...  5.73 us
    ppermute x4, waiting for transfers between devices, on_device(): lax.ppermute(x, 'inst', perms[n])  4.89 us
    pallas_call x1, Pallas kernels, on_device(): pl.pallas_call(functools.partial(attend_kernel, shifts, groups), out_shap...  2.06 us
    ppermute x3, waiting for transfers between devices, on_device(): lax.ppermute(x, 'tp', [(i, (i + 2 * (d + 1)) % parts) for i in range(part...  1.2 us
    pallas_call x1, Pallas kernels, on_device(): pl.pallas_call(functools.partial(place_kernel, plan), out_shape=shape(cac...  1 us
    pallas_call x1, Pallas kernels, on_device(): pl.pallas_call(project_kernel, out_shape=[shape((chips, 2 * REQS, width))...  0.86 us
    pallas_call x1, Pallas kernels, on_device(): pl.pallas_call(own_kernel, out_shape=shape((chips, 2 * REQS, width), jnp....  0.86 us
  transfers between devices with their start and end apart: 8, of which 3 were waited for; matrix products, arithmetic and copies ran while one was open for 0% of the time, Pallas kernels for 10%

profile of v8, /device:TPU:24, one launch (start us, length us, event | category | flops | bytes accessed | tf_op | source)
XLA Modules:
  0.0 28.1 jit_solution(10459653232695289293)
XLA Ops:
  0.6 0.0 copy-start
  0.6 2.1 %attend.1 = (bf16[144,128]{1,0:T(8,128)(2,1)S(1)}, bf16[656,128]{1,0:T(8,128)(2,1)S(1)}, bf16[384,128]{1,0:T(8,128)(2,1)S(1)}, bf16[896,128]{1,0:T(8,128)(2,1)S(...) custom-call(s32[128]{0:T(128)} %targets_hbm.1, s32[128]{0:T(128)} %lengths_hbm.1, ...), custom_call_target="tpu_custom_call" | custom-call | flops 10000000000 | bytes 1000000 | tf_op jit(solution)/shard_map/attend/pallas_call | solution.py:224
  2.7 1.7 %collective-permute-start.2 = (bf16[656,128]{1,0:T(8,128)(2,1)S(1)}, bf16[656,128]{1,0:T(8,128)(2,1)S(1)}, u32[]{:S(2)}, u32[]{:S(2)}) collective-permute-start(bf16[656,128]{1,0:T(8,128)(2,1)S(1)} %get-tuple-element.22), channel_id=1, source_target_pairs={{0,8},{8,16},{16,24},{24,32},{32,40},{40,48},{48,56},{56,64},{64,7... | collective-permute-start | bytes 503816 | tf_op jit(solution)/shard_map/ppermute | solution.py:245
  4.4 6.3 %collective-permute-start.3 = (bf16[144,128]{1,0:T(8,128)(2,1)S(1)}, bf16[144,128]{1,0:T(8,128)(2,1)S(1)}, u32[]{:S(2)}, u32[]{:S(2)}) collective-permute-start(bf16[144,128]{1,0:T(8,128)(2,1)S(1)} %get-tuple-element.23), channel_id=1, source_target_pairs={{0,128},{8,136},{16,144},{24,152},{32,160},{40,168},{48,176},{56,1... | collective-permute-start | bytes 110600 | tf_op jit(solution)/shard_map/ppermute | solution.py:245
  10.7 1.6 %collective-permute-start = (bf16[384,128]{1,0:T(8,128)(2,1)S(1)}, bf16[384,128]{1,0:T(8,128)(2,1)S(1)}, u32[]{:S(2)}, u32[]{:S(2)}) collective-permute-start(bf16[384,128]{1,0:T(8,128)(2,1)S(1)} %get-tuple-element.20), channel_id=1, source_target_pairs={{0,8},{8,16},{16,24},{24,32},{32,40},{40,48},{48,56},{56,64},{64,7... | collective-permute-start | bytes 294920 | tf_op jit(solution)/shard_map/ppermute | solution.py:245
  12.2 0.0 collective-permute-start.1
  12.2 4.9 %collective-permute-done.3.far_ref = bf16[144,128]{1,0:T(8,128)(2,1)S(1)} collective-permute-done((bf16[144,128]{1,0:T(8,128)(2,1)S(1)}, bf16[144,128]{1,0:T(8,128)(2,1)S(1)}, u32[]{:S(2)}, u32[]{:S(2)}) %collective-permute-start.3) | collective-permute-done | bytes 36896 | tf_op jit(solution)/shard_map/ppermute | solution.py:245
  17.1 0.0 collective-permute-done.2.near_ref
  17.1 0.0 copy-done
  17.1 0.9 %project.1 = (bf16[4,8,640]{2,1,0:T(8,128)(2,1)S(1)}, bf16[8,1024]{1,0:T(8,128)(2,1)S(1)}) custom-call(f32[8,128]{1,0:T(8,128)S(1)} %get-tuple-element.19.places_ref, f32[64,128]{1,0:T(8,128)S(1)} %get-tuple-element.25.att_ref, bf16[656,128]{1,0:T(8,128)(2,1)S(1)} %collective-permute-done.2.near_ref, bf16[144,128]{1,0:T(8,128)(2,1)S(1)} %collective-permute-done.3.far_ref, ...), custom_call_target="tpu_custom_call" | custom-call | flops 4000000000 | bytes 1000000 | tf_op jit(solution)/shard_map/project/pallas_call | solution.py:249
  18.0 0.1 collective-permute-start.4
  18.1 0.9 %own.1.mine_ref = f32[4,8,640]{2,1,0:T(8,128)S(1)} custom-call(bf16[8,1024]{1,0:T(8,128)(2,1)S(1)} %get-tuple-element.26.lhs, bf16[1024,5120]{1,0:T(8,128)(2,1)S(1)} %copy-done), custom_call_target="tpu_custom_call" | custom-call | flops 1000000000 | bytes 1000000 | tf_op jit(solution)/shard_map/own/pallas_call | solution.py:258
  18.9 0.3 %collective-permute-done.4.theirs_ref = bf16[4,8,640]{2,1,0:T(8,128)(2,1)S(1)} collective-permute-done((bf16[4,8,640]{2,1,0:T(8,128)(2,1)S(1)}, bf16[4,8,640]{2,1,0:T(8,128)(2,1)S(1)}, u32[]{:S(2)}, u32[]{:S(2)}) %collective-permute-start.4) | collective-permute-done | bytes 40992 | tf_op jit(solution)/shard_map/ppermute | solution.py:267
  19.3 1.6 %collective-permute-start.5 = (bf16[8,640]{1,0:T(8,128)(2,1)S(1)}, bf16[8,640]{1,0:T(8,128)(2,1)S(1)}, u32[]{:S(2)}, u32[]{:S(2)}) collective-permute-start(bf16[8,640]{1,0:T(8,128)(2,1)S(1)} %get-tuple-element.29), channel_id=1, source_target_pairs={{0,2},{1,3},{2,4},{3,5},{4,6},{5,7},{6,0},{7,1},{8,10},{9,11},{10,... | collective-permute-start | bytes 30728 | tf_op jit(solution)/shard_map/ppermute | solution.py:277
  20.9 2.7 %collective-permute-start.6 = (bf16[8,640]{1,0:T(8,128)(2,1)S(1)}, bf16[8,640]{1,0:T(8,128)(2,1)S(1)}, u32[]{:S(2)}, u32[]{:S(2)}) collective-permute-start(bf16[8,640]{1,0:T(8,128)(2,1)S(1)} %get-tuple-element.30), channel_id=1, source_target_pairs={{0,4},{1,5},{2,6},{3,7},{4,0},{5,1},{6,2},{7,3},{8,12},{9,13},{10,... | collective-permute-start | bytes 30728 | tf_op jit(solution)/shard_map/ppermute | solution.py:277
  23.6 1.4 %collective-permute-start.7 = (bf16[8,640]{1,0:T(8,128)(2,1)S(1)}, bf16[8,640]{1,0:T(8,128)(2,1)S(1)}, u32[]{:S(2)}, u32[]{:S(2)}) collective-permute-start(bf16[8,640]{1,0:T(8,128)(2,1)S(1)} %get-tuple-element.31), channel_id=1, source_target_pairs={{0,6},{1,7},{2,0},{3,1},{4,2},{5,3},{6,4},{7,5},{8,14},{9,15},{10,... | collective-permute-start | bytes 30728 | tf_op jit(solution)/shard_map/ppermute | solution.py:277
  25.0 1.0 %place.1.rest_2_ = bf16[2,4,512,128]{3,2,1,0:T(8,128)(2,1)} custom-call(f32[8,128]{1,0:T(8,128)S(1)} %get-tuple-element.19.places_ref, bf16[656,128]{1,0:T(8,128)(2,1)S(1)} %collective-permute-done.2.near_ref, bf16[144,128]{1,0:T(8,128)(2,1)S(1)} %collective-permute-done.3.far_ref, bf16[2,4,512,128]{3,2,1,0:T(8,128)(2,1)S(1)} %get-tuple-element.24.stored), custom_call_target="tpu_custom_call" | custom-call | flops 500000000 | bytes 1000000 | tf_op jit(solution)/shard_map/place/pallas_call | solution.py:284
  26.0 0.0 collective-permute-done.rest_0_
  26.0 0.0 collective-permute-done.5.rest_4_
  26.1 0.0 collective-permute-done.6.rest_5_
  26.1 1.2 %collective-permute-done.7.rest_6_ = bf16[8,640]{1,0:T(8,128)(2,1)S(1)} collective-permute-done((bf16[8,640]{1,0:T(8,128)(2,1)S(1)}, bf16[8,640]{1,0:T(8,128)(2,1)S(1)}, u32[]{:S(2)}, u32[]{:S(2)}) %collective-permute-start.7) | collective-permute-done | bytes 10272 | tf_op jit(solution)/shard_map/ppermute | solution.py:277
  27.3 0.0 collective-permute-done.1.rest_1_
  27.3 0.8 %finish.1 = (bf16[2,4,512,128]{3,2,1,0:T(8,128)(2,1)}, bf16[4,640]{1,0:T(4,128)(2,1)}, bf16[4,640]{1,0:T(4,128)(2,1)}) custom-call(f32[8,128]{1,0:T(8,128)S(1)} %get-tuple-element.19.places_ref, bf16[384,128]{1,0:T(8,128)(2,1)S(1)} %collective-permute-done.rest_0_, ...), custom_call_target="tpu_custom_call", output_to_operand_aliasing={{0}: (3, {})} | custom-call | tf_op jit(solution)/shard_map/finish/pallas_call | solution.py:303
  (1 shorter events, 0.0 us)
Async XLA Ops:
  0.6 16.5 %copy-start = (bf16[1024,5120]{1,0:T(8,128)(2,1)S(1)}, bf16[1024,5120]{1,0:T(8,128)(2,1)}, u32[]{:S(2)}) copy-start(bf16[1024,5120]{1,0:T(8,128)(2,1)} %weight_ref.3) | copy-start | bytes 31457284
  2.7 14.4 %collective-permute-start.2 = (bf16[656,128]{1,0:T(8,128)(2,1)S(1)}, bf16[656,128]{1,0:T(8,128)(2,1)S(1)}, u32[]{:S(2)}, u32[]{:S(2)}) collective-permute-start(bf16[656,128]{1,0:T(8,128)(2,1)S(1)} %get-tuple-element.22), channel_id=1, source_target_pairs={{0,8},{8,16},{16,24},{24,32},{32,40},{40,48},{48,56},{56,64},{64,7... | collective-permute-start | bytes 503816 | tf_op jit(solution)/shard_map/ppermute | solution.py:245
  4.4 12.7 %collective-permute-start.3 = (bf16[144,128]{1,0:T(8,128)(2,1)S(1)}, bf16[144,128]{1,0:T(8,128)(2,1)S(1)}, u32[]{:S(2)}, u32[]{:S(2)}) collective-permute-start(bf16[144,128]{1,0:T(8,128)(2,1)S(1)} %get-tuple-element.23), channel_id=1, source_target_pairs={{0,128},{8,136},{16,144},{24,152},{32,160},{40,168},{48,176},{56,1... | collective-permute-start | bytes 110600 | tf_op jit(solution)/shard_map/ppermute | solution.py:245
  10.7 15.4 %collective-permute-start = (bf16[384,128]{1,0:T(8,128)(2,1)S(1)}, bf16[384,128]{1,0:T(8,128)(2,1)S(1)}, u32[]{:S(2)}, u32[]{:S(2)}) collective-permute-start(bf16[384,128]{1,0:T(8,128)(2,1)S(1)} %get-tuple-element.20), channel_id=1, source_target_pairs={{0,8},{8,16},{16,24},{24,32},{32,40},{40,48},{48,56},{56,64},{64,7... | collective-permute-start | bytes 294920 | tf_op jit(solution)/shard_map/ppermute | solution.py:245
  12.2 15.0 %collective-permute-start.1 = (bf16[896,128]{1,0:T(8,128)(2,1)S(1)}, bf16[896,128]{1,0:T(8,128)(2,1)S(1)}, u32[]{:S(2)}, u32[]{:S(2)}) collective-permute-start(bf16[896,128]{1,0:T(8,128)(2,1)S(1)} %get-tuple-element.21), channel_id=1, source_target_pairs={{0,128},{8,136},{16,144},{24,152},{32,160},{40,168},{48,176},{56,1... | collective-permute-start | bytes 688136 | tf_op jit(solution)/shard_map/ppermute | solution.py:245
  18.0 1.3 %collective-permute-start.4 = (bf16[4,8,640]{2,1,0:T(8,128)(2,1)S(1)}, bf16[4,8,640]{2,1,0:T(8,128)(2,1)S(1)}, u32[]{:S(2)}, u32[]{:S(2)}) collective-permute-start(bf16[4,8,640]{2,1,0:T(8,128)(2,1)S(1)} %get-tuple-element.27), channel_id=1, source_target_pairs={{0,1},{1,0},{2,3},{3,2},{4,5},{5,4},{6,7},{7,6},{8,9},{9,8},{10,11... | collective-permute-start | bytes 122888 | tf_op jit(solution)/shard_map/ppermute | solution.py:267
  19.3 6.8 %collective-permute-start.5 = (bf16[8,640]{1,0:T(8,128)(2,1)S(1)}, bf16[8,640]{1,0:T(8,128)(2,1)S(1)}, u32[]{:S(2)}, u32[]{:S(2)}) collective-permute-start(bf16[8,640]{1,0:T(8,128)(2,1)S(1)} %get-tuple-element.29), channel_id=1, source_target_pairs={{0,2},{1,3},{2,4},{3,5},{4,6},{5,7},{6,0},{7,1},{8,10},{9,11},{10,... | collective-permute-start | bytes 30728 | tf_op jit(solution)/shard_map/ppermute | solution.py:277
  20.9 5.2 %collective-permute-start.6 = (bf16[8,640]{1,0:T(8,128)(2,1)S(1)}, bf16[8,640]{1,0:T(8,128)(2,1)S(1)}, u32[]{:S(2)}, u32[]{:S(2)}) collective-permute-start(bf16[8,640]{1,0:T(8,128)(2,1)S(1)} %get-tuple-element.30), channel_id=1, source_target_pairs={{0,4},{1,5},{2,6},{3,7},{4,0},{5,1},{6,2},{7,3},{8,12},{9,13},{10,... | collective-permute-start | bytes 30728 | tf_op jit(solution)/shard_map/ppermute | solution.py:277
  23.6 3.7 %collective-permute-start.7 = (bf16[8,640]{1,0:T(8,128)(2,1)S(1)}, bf16[8,640]{1,0:T(8,128)(2,1)S(1)}, u32[]{:S(2)}, u32[]{:S(2)}) collective-permute-start(bf16[8,640]{1,0:T(8,128)(2,1)S(1)} %get-tuple-element.31), channel_id=1, source_target_pairs={{0,6},{1,7},{2,0},{3,1},{4,2},{5,3},{6,4},{7,5},{8,14},{9,15},{10,... | collective-permute-start | bytes 30728 | tf_op jit(solution)/shard_map/ppermute | solution.py:277
